TPU v7x, 32 devices: a whole 2x2x4 slice. The times are simulated.
32 devices in a mesh: parts: 1, wide: 16 (over z, y, x), narrow: 2 (over core).
Axes of the slice: x: 2, y: 2, z: 4, core: 2. Of those that a mesh axis runs over, the one named last changes fastest.
Arguments:
- tokens: bfloat16 [4096, 3584], P(('parts', 'wide', 'narrow')), may hold values from -6 to 6
- grad_out: bfloat16 [4096, 3584], P(('parts', 'wide', 'narrow')), may hold values from -6 to 6
- expert_ids: int32 [4096], P(('parts', 'wide', 'narrow')), may hold values from 0 to 7, as said below
- combine: float32 [4096], P(('parts', 'wide', 'narrow')), may hold values from 0.1 to 1
- w_gate: bfloat16 [2, 3584, 4096], P('narrow', None, 'wide'), may hold values from -0.09375 to 0.09375
- w_up: bfloat16 [2, 3584, 4096], P('narrow', None, 'wide'), may hold values from -0.09375 to 0.09375
- w_down: bfloat16 [2, 4096, 3584], P('narrow', 'wide'), may hold values from -0.1875 to 0.1875
Outputs:
- token_grad: bfloat16 [4096, 3584], P(('parts', 'wide', 'narrow'))
- prob_grad: float32 [4096], P(('parts', 'wide', 'narrow'))
Inputs may be any that keep to these rules, and one draw needn't show every extreme that they name: `expert_ids`: among the 128 tokens of each device, every expert is chosen at most 32 times; one expert, the same for all devices, is chosen exactly 32 times on every device.
All inputs are finite; a program needn't handle non-finite values.
Results may differ from a plain program's by a relative error of at most 0.0051.
Values may be sent and summed in bfloat16 or wider, within the bound.
No kernel may reach another device: no remote copies, remote signals or barrier semaphores. Data moves between devices by JAX's collectives and lax.ppermute only.
A program may use at most 128 MiB of HBM per device.

v0:
```python
import jax
import jax.numpy as jnp
from jax import lax
from jax.sharding import PartitionSpec as P

SHARDS = 4


def silu_parts(gate):
    sigma = jax.nn.sigmoid(gate)
    return (gate * sigma, sigma * (1.0 + gate * (1.0 - sigma)))


def times_transposed(left, right):
    return lax.dot_general(
        left, right, (((1,), (1,)), ((), ())), preferred_element_type=jnp.float32
    )


def shards(tokens, grad_out, expert_ids, combine, w_gate, w_up, w_down):
    wide = lax.axis_size("wide")
    narrow = lax.axis_size("narrow")
    devices = wide * narrow
    blocks = wide // SHARDS
    experts = blocks * narrow
    count = tokens.shape[0]
    width = tokens.shape[1]
    cap = 2 * count // experts
    gate_w = w_gate[0]
    up_w = w_up[0]
    down_w = w_down[0]
    hits = (expert_ids[:, None] == jnp.arange(experts, dtype=jnp.int32)[None, :]).astype(
        jnp.float32
    )
    earlier = (jnp.arange(count)[:, None] > jnp.arange(count)[None, :]).astype(jnp.float32)
    before = jnp.dot(earlier, hits, precision=lax.Precision.HIGHEST)
    slot = jnp.sum(before * hits, axis=1).astype(jnp.int32)
    place = expert_ids * cap + slot
    select = (jnp.arange(experts * cap, dtype=jnp.int32)[:, None] == place[None, :]).astype(
        jnp.bfloat16
    )
    packed_x = jnp.dot(select, tokens, preferred_element_type=jnp.float32).astype(jnp.bfloat16)
    packed_g = jnp.dot(select, grad_out, preferred_element_type=jnp.float32).astype(jnp.bfloat16)

    def spread(packed):
        shaped = packed.reshape(narrow, blocks, cap, width).transpose(1, 0, 2, 3)
        shaped = jnp.broadcast_to(shaped[:, None], (blocks, SHARDS, narrow, cap, width))
        return shaped.reshape(wide, narrow, cap, width)

    outgoing_x = spread(packed_x)
    outgoing_g = spread(packed_g)
    items = outgoing_x.shape[2]
    flat_x = outgoing_x.reshape(devices, items, width)
    flat_g = outgoing_g.reshape(devices, items, width)
    rows_x = lax.all_to_all(flat_x, ("wide", "narrow"), split_axis=0, concat_axis=0, tiled=True)
    rows_g = lax.all_to_all(flat_g, ("wide", "narrow"), split_axis=0, concat_axis=0, tiled=True)
    leading = rows_x.shape[:-1]
    flat_x = rows_x.reshape(-1, width)
    flat_g = rows_g.reshape(-1, width)
    gate = jnp.dot(flat_x, gate_w, preferred_element_type=jnp.float32)
    up = jnp.dot(flat_x, up_w, preferred_element_type=jnp.float32)
    back = times_transposed(flat_g, down_w)
    act, slope = silu_parts(gate)
    prob_part = jnp.sum(act * up * back, axis=1)
    gate_grad = (back * up * slope).astype(jnp.bfloat16)
    up_grad = (back * act).astype(jnp.bfloat16)
    input_part = times_transposed(gate_grad, gate_w) + times_transposed(up_grad, up_w)
    input_part, prob_part = (input_part.reshape(leading + (width,)), prob_part.reshape(leading))
    returned = lax.all_to_all(
        input_part, ("wide", "narrow"), split_axis=0, concat_axis=0, tiled=True
    )
    prob_back = lax.all_to_all(
        prob_part, ("wide", "narrow"), split_axis=0, concat_axis=0, tiled=True
    )
    returned = returned.reshape(wide, narrow, items, width)
    prob_back = prob_back.reshape(wide, narrow, items)
    summed = jnp.sum(returned.reshape(blocks, SHARDS, narrow, cap, width), axis=1).reshape(
        blocks * narrow * cap, width
    )
    prob_sum = jnp.sum(prob_back.reshape(blocks, SHARDS, narrow, cap), axis=1).reshape(
        blocks * narrow * cap
    )
    index_rows = (expert_ids % blocks * narrow + expert_ids // blocks) * cap + slot
    token_grad = (combine[:, None] * summed[index_rows]).astype(jnp.bfloat16)
    prob_grad = prob_sum[index_rows]
    return (token_grad, prob_grad)


def solution(mesh):
    in_specs = (
        P(("parts", "wide", "narrow"), None),
        P(("parts", "wide", "narrow"), None),
        P(("parts", "wide", "narrow")),
        P(("parts", "wide", "narrow")),
        P("narrow", None, "wide"),
        P("narrow", None, "wide"),
        P("narrow", "wide", None),
    )
    out_specs = (P(("parts", "wide", "narrow"), None), P(("parts", "wide", "narrow")))
    return jax.shard_map(shards, mesh=mesh, in_specs=in_specs, out_specs=out_specs, check_vma=False)
```

profile of v0, /device:TPU:19, one launch (start us, length us, event | category | flops | bytes accessed | tf_op | source)
XLA Modules:
  0.0 711.0 jit_solution(11297305080309936204)
XLA Ops:
  0.6 0.0 copy-start
  0.6 1.0 fusion.9
  1.6 0.7 compare_select_fusion
  2.3 1.8 convolution_convert_fusion
  4.1 0.2 copy.19
  4.3 3.8 broadcast_in_dim.7
  8.1 6.3 all-to-all-start.1
  14.4 0.0 copy-done.4
  14.4 0.6 convolution_convert_fusion.1
  15.0 1.4 copy.18
  16.5 155.5 %all-to-all-done.1 = bf16[32,32,3584]{2,1,0:T(8,128)(2,1)} async-done(((bf16[32,32,3584]{2,1,0:T(8,128)(2,1)}), bf16[32,32,3584]{2,1,0:T(8,128)(2,1)}, u32[]{:S(2)}, u32[]{:S(2)}) %all-to-all-start.1) | async-done | bytes 7340064 | tf_op jit(solution)/shard_map/all_to_all | solution.py:55
  172.0 5.2 broadcast_in_dim.6
  177.2 9.1 %all-to-all-start = ((bf16[32,32,3584]{2,1,0:T(8,128)(2,1)}), bf16[32,32,3584]{2,1,0:T(8,128)(2,1)}, u32[]{:S(2)}, u32[]{:S(2)}) async-start(bf16[32,32,3584]{2,1,0:T(8,128)(2,1)} %bitcast.37), calls=%async_computation | async-start | bytes 14680064 | tf_op jit(solution)/shard_map/all_to_all | solution.py:56
  186.4 0.0 copy-start.3
  186.4 5.3 fusion.2
  191.7 6.2 fusion.5
  197.9 146.0 %all-to-all-done = bf16[32,32,3584]{2,1,0:T(8,128)(2,1)} async-done(((bf16[32,32,3584]{2,1,0:T(8,128)(2,1)}), bf16[32,32,3584]{2,1,0:T(8,128)(2,1)}, u32[]{:S(2)}, u32[]{:S(2)}) %all-to-all-start) | async-done | bytes 7340064 | tf_op jit(solution)/shard_map/all_to_all | solution.py:56
  344.0 6.9 multiply_reduce_fusion
  350.9 0.7 all_to_all.18
  351.6 8.2 %all-to-all-start.3 = ((f32[32,1,32]{2,1,0:T(1,128)}), f32[32,1,32]{2,1,0:T(1,128)S(1)}, u32[]{:S(2)}, u32[]{:S(2)}) async-start(f32[32,1,32]{2,1,0:T(1,128)} %all_to_all.18), calls=%async_computation.3 | async-start | bytes 32768 | tf_op jit(solution)/shard_map/all_to_all | solution.py:72
  359.8 4.1 fusion
  363.8 0.0 copy-done.2
  363.8 9.1 %convolution_add_fusion = f32[1024,3584]{1,0:T(8,128)} fusion(f32[1024,3584]{1,0:T(8,128)S(1)} %fusion, bf16[1,3584,256]{2,1,0:T(8,128)(2,1)} %param.12, f32[1024,256]{0,1:T(8,128)S(1)} %copy-done.2, f32[1024,256]{0,1:T(8,128)S(1)} %fusion.2), kind=kOutput, calls=%fused_computation.2 | convolution fusion | flops 1884291072 | bytes 33292288 | tf_op jit(solution)/shard_map/dot_general | solution.py:15
  372.9 0.0 all-to-all-done.3
  372.9 5.9 all-to-all-start.2
  378.8 0.1 reshape.41
  378.9 1.8 gather_fusion.1
  380.7 313.5 %all-to-all-done.2 = f32[32,32,3584]{2,1,0:T(8,128)} async-done(((f32[32,32,3584]{2,1,0:T(8,128)}), f32[32,32,3584]{2,1,0:T(8,128)}, u32[]{:S(2)}, u32[]{:S(2)}) %all-to-all-start.2) | async-done | bytes 14680096 | tf_op jit(solution)/shard_map/all_to_all | solution.py:69
  694.2 8.8 %reduce_sum.37 = f32[4,2,32,3584]{3,2,1,0:T(8,128)} reduce(f32[4,4,2,32,3584]{4,3,2,1,0:T(8,128)} %bitcast.12, f32[]{:T(128)} %constant.30.clone.1), dimensions={1}, to_apply=%region_1.0 | reduce | flops 2752512 | bytes 18350084 | tf_op jit(solution)/shard_map/reduce_sum | solution.py:77
  703.0 5.4 gather_fusion
  708.4 2.6 multiply_convert_fusion
  711.0 0.0 copy-done.1
  (9 shorter events, 0.0 us)
Async XLA Ops:
  0.6 185.8 %copy-start = (bf16[1,3584,256]{2,1,0:T(8,128)(2,1)S(1)}, bf16[1,3584,256]{2,1,0:T(8,128)(2,1)}, u32[]{:S(2)}) copy-start(bf16[1,3584,256]{2,1,0:T(8,128)(2,1)} %param.11) | copy-start | bytes 5505028
  8.1 6.3 copy-start.4
  8.1 163.9 %all-to-all-start.1 = ((bf16[32,32,3584]{2,1,0:T(8,128)(2,1)}), bf16[32,32,3584]{2,1,0:T(8,128)(2,1)}, u32[]{:S(2)}, u32[]{:S(2)}) async-start(bf16[32,32,3584]{2,1,0:T(8,128)(2,1)} %bitcast.36), calls=%async_computation.1 | async-start | bytes 14680064 | tf_op jit(solution)/shard_map/all_to_all | solution.py:55
  177.2 166.7 %all-to-all-start = ((bf16[32,32,3584]{2,1,0:T(8,128)(2,1)}), bf16[32,32,3584]{2,1,0:T(8,128)(2,1)}, u32[]{:S(2)}, u32[]{:S(2)}) async-start(bf16[32,32,3584]{2,1,0:T(8,128)(2,1)} %bitcast.37), calls=%async_computation | async-start | bytes 14680064 | tf_op jit(solution)/shard_map/all_to_all | solution.py:56
  186.4 5.3 copy-start.3
  351.6 21.3 %all-to-all-start.3 = ((f32[32,1,32]{2,1,0:T(1,128)}), f32[32,1,32]{2,1,0:T(1,128)S(1)}, u32[]{:S(2)}, u32[]{:S(2)}) async-start(f32[32,1,32]{2,1,0:T(1,128)} %all_to_all.18), calls=%async_computation.3 | async-start | bytes 32768 | tf_op jit(solution)/shard_map/all_to_all | solution.py:72
  359.8 4.1 copy-start.2
  372.9 321.3 %all-to-all-start.2 = ((f32[32,32,3584]{2,1,0:T(8,128)}), f32[32,32,3584]{2,1,0:T(8,128)}, u32[]{:S(2)}, u32[]{:S(2)}) async-start(f32[32,32,3584]{2,1,0:T(8,128)} %bitcast.34), calls=%async_computation.2 | async-start | bytes 29360128 | tf_op jit(solution)/shard_map/all_to_all | solution.py:69
  703.0 5.4 copy-start.5
  703.0 8.0 %copy-start.1 = (bf16[1,3584,256]{2,1,0:T(8,128)(2,1)S(1)}, bf16[1,3584,256]{2,1,0:T(8,128)(2,1)}, u32[]{:S(2)}) copy-start(bf16[1,3584,256]{2,1,0:T(8,128)(2,1)} %param.11) | copy-start | bytes 5505028
where the time goes:
time: 723 us; the launch traced here: 711 us
  waiting for transfers between devices  615 us (85%)
  matrix products  35 us (5%)
  starting transfers between devices  29.4 us (4%)
  local copies, waits for them, and re-layouts  18.6 us (3%)
  other arithmetic  12.1 us (2%)
    all_to_all x1, waiting for transfers between devices, shards(): lax.all_to_all(input_part, ('wide', 'narrow'), split_axis=0, concat_axis=...  313 us
    all_to_all x1, waiting for transfers between devices, shards(): lax.all_to_all(flat_x, ('wide', 'narrow'), split_axis=0, concat_axis=0, t...  156 us
    all_to_all x1, waiting for transfers between devices, shards(): lax.all_to_all(flat_g, ('wide', 'narrow'), split_axis=0, concat_axis=0, t...  146 us
    dot_general x3, matrix products, times_transposed(): lax.dot_general(left, right, (((1,), (1,)), ((), ())), preferred_element_...  20.1 us
  transfers between devices with their start and end apart: 4, of which 3 were waited for; matrix products, arithmetic and copies ran while one was open for 4% of the time, Pallas kernels for 0%

commit v1 on v0

v1 whole, which is shorter than its diff:
```python
import jax
import jax.numpy as jnp
from jax import lax
from jax.sharding import PartitionSpec as P

SHARDS = 4
AXES = ("wide", "narrow")


def silu_parts(gate):
    sigma = jax.nn.sigmoid(gate)
    return (gate * sigma, sigma * (1.0 + gate * (1.0 - sigma)))


def times(left, right):
    return jnp.dot(left, right, preferred_element_type=jnp.float32)


def times_transposed(left, right):
    return lax.dot_general(
        left, right, (((1,), (1,)), ((), ())), preferred_element_type=jnp.float32
    )


def shards(tokens, grad_out, expert_ids, combine, w_gate, w_up, w_down):
    wide = lax.axis_size("wide")
    narrow = lax.axis_size("narrow")
    blocks = wide // SHARDS
    experts = blocks * narrow
    count, width = tokens.shape
    cap = 2 * count // experts
    block = lax.axis_index("wide") // SHARDS
    core = lax.axis_index("narrow")

    def permute(value, target):
        pairs = []
        for w in range(wide):
            for c in range(narrow):
                b, s, n = target(w // SHARDS, w % SHARDS, c)
                pairs.append((w * narrow + c, (b * SHARDS + s) * narrow + n))
        return lax.ppermute(value, AXES, pairs)

    def swap_weights(value):
        return permute(value, lambda b, s, c: (b, s ^ (1 if c == 0 else 2), c))

    def swap_rows(value):
        return permute(value, lambda b, s, c: (b, s ^ (2 if c == 0 else 1), c))

    def send(value, k, m):
        if k == 0 and m == 0:
            return value
        return permute(value, lambda b, s, c: ((b + k) % blocks, s, (c + m) % narrow))

    def give_back(value, k, m):
        if k == 0 and m == 0:
            return value
        return permute(value, lambda b, s, c: ((b - k) % blocks, s, (c - m) % narrow))

    gate_w = jnp.concatenate([w_gate[0], swap_weights(w_gate[0])], axis=1)
    up_w = jnp.concatenate([w_up[0], swap_weights(w_up[0])], axis=1)
    down_w = jnp.concatenate([w_down[0], swap_weights(w_down[0])], axis=0)

    hits = (expert_ids[:, None] == jnp.arange(experts, dtype=jnp.int32)[None, :]).astype(
        jnp.float32
    )
    earlier = (jnp.arange(count)[:, None] > jnp.arange(count)[None, :]).astype(jnp.float32)
    before = jnp.dot(earlier, hits, precision=lax.Precision.HIGHEST)
    slot = jnp.sum(before * hits, axis=1).astype(jnp.int32)
    shift = (expert_ids % blocks - block + blocks) % blocks
    turn = (expert_ids // blocks - core + narrow) % narrow
    place = (shift * narrow + turn) * cap + slot
    select = jnp.arange(experts * cap, dtype=jnp.int32)[:, None] == place[None, :]
    packed_x = times(select.astype(jnp.bfloat16), tokens).astype(jnp.bfloat16)
    packed_g = times(select.astype(jnp.bfloat16), grad_out).astype(jnp.bfloat16)
    packed = jnp.stack(
        [packed_x.reshape(experts, cap, width), packed_g.reshape(experts, cap, width)], axis=1
    )

    order = sorted(range(blocks), key=lambda k: (k != 0, -min(k, blocks - k), k))
    rows = {}
    for k in order:
        own = [send(packed[k * narrow + m], k, m) for m in range(narrow)]
        other = [swap_rows(part) for part in own]
        rows[k] = (own, other)

    back_rows = {}
    back_probs = {}
    half = narrow * cap
    for k in order:
        own, other = rows[k]
        x = jnp.concatenate([part[0] for part in own + other], axis=0)
        g = jnp.concatenate([part[1] for part in own + other], axis=0)
        gate = times(x, gate_w)
        up = times(x, up_w)
        back = times_transposed(g, down_w)
        act, slope = silu_parts(gate)
        prob_part = jnp.sum(act * up * back, axis=1)
        gate_grad = (back * up * slope).astype(jnp.bfloat16)
        up_grad = (back * act).astype(jnp.bfloat16)
        partial = times_transposed(gate_grad, gate_w) + times_transposed(up_grad, up_w)
        mine = partial[:half] + swap_rows(partial[half:].astype(jnp.bfloat16)).astype(jnp.float32)
        mine = mine.astype(jnp.bfloat16)
        prob = prob_part[:half] + swap_rows(prob_part[half:])
        for m in range(narrow):
            back_rows[k * narrow + m] = give_back(mine[m * cap : (m + 1) * cap], k, m)
            back_probs[k * narrow + m] = give_back(prob[m * cap : (m + 1) * cap], k, m)

    returned = jnp.concatenate([back_rows[i] for i in range(experts)], axis=0)
    probs = jnp.concatenate([back_probs[i] for i in range(experts)], axis=0)
    token_grad = combine[:, None] * times(select.T.astype(jnp.bfloat16), returned)
    prob_grad = jnp.sum(jnp.where(select, probs[:, None], 0.0), axis=0)
    return (token_grad.astype(jnp.bfloat16), prob_grad)


def solution(mesh):
    in_specs = (
        P(("parts", "wide", "narrow"), None),
        P(("parts", "wide", "narrow"), None),
        P(("parts", "wide", "narrow")),
        P(("parts", "wide", "narrow")),
        P("narrow", None, "wide"),
        P("narrow", None, "wide"),
        P("narrow", "wide", None),
    )
    out_specs = (P(("parts", "wide", "narrow"), None), P(("parts", "wide", "narrow")))
    return jax.shard_map(shards, mesh=mesh, in_specs=in_specs, out_specs=out_specs, check_vma=False)
```

time: 723 us -> 236 us (0.33); the launches traced: 711 us -> 236 us
  waiting for transfers between devices: 615 us -> 141 us
  starting transfers between devices: 29.4 us -> 57 us
  local copies, waits for them, and re-layouts: 18.6 us -> 6.3 us
  matrix products: 35 us -> 25 us
    all_to_all x4 -> x0, waiting for transfers between devices: 615 us -> none  [the longest x1 313 us: shards(): lax.all_to_all(input_part, ('wide', 'narrow'), split_axis=0, concat_axis=...]
    ppermute x0 -> x40, waiting for transfers between devices: none -> 141 us  [permute(): return lax.ppermute(value, AXES, pairs)]
    ppermute x0 -> x40, starting transfers between devices: none -> 57 us  [permute(): return lax.ppermute(value, AXES, pairs)]
    all_to_all x4 -> x0, starting transfers between devices: 29.4 us -> none  [the longest x1 9.13 us: shards(): lax.all_to_all(flat_g, ('wide', 'narrow'), split_axis=0, concat_axis=0, t...]
    broadcast_in_dim x2 -> x0, local copies, waits for them, and re-layouts: 9.09 us -> none  [spread(): jnp.broadcast_to(shaped[:, None], (blocks, SHARDS, narrow, cap, width))]
    reduce_sum x2 -> x1, other arithmetic: 8.86 us -> 0.63 us  [shards(): prob_grad = jnp.sum(jnp.where(select, probs[:, None], 0.0), axis=0)]
    dot_general x3 -> x12, matrix products: 20.1 us -> 16.1 us  [times_transposed(): lax.dot_general(left, right, (((1,), (1,)), ((), ())), preferred_element_...]
  transfers between devices with their start and end apart: 4 -> 40, of which waited for: 3 -> 23; matrix products, arithmetic and copies ran while one was open for 4% -> 11% of each run, Pallas kernels for 0% -> 0%
where the time goes in v1:
time: 236 us
  waiting for transfers between devices  141 us (60%)
  starting transfers between devices  57 us (24%)
  matrix products  25 us (11%)
  local copies, waits for them, and re-layouts  6.3 us (3%)
  other arithmetic  5.08 us (2%)
    ppermute x40, waiting for transfers between devices, permute(): return lax.ppermute(value, AXES, pairs)  141 us
    ppermute x40, starting transfers between devices, permute(): return lax.ppermute(value, AXES, pairs)  57 us
    dot_general x12, matrix products, times_transposed(): lax.dot_general(left, right, (((1,), (1,)), ((), ())), preferred_element_...  16.1 us
    dot_general x11, matrix products, times(): return jnp.dot(left, right, preferred_element_type=jnp.float32)  7.96 us
  transfers between devices with their start and end apart: 40, of which 23 were waited for; matrix products, arithmetic and copies ran while one was open for 11% of the time, Pallas kernels for 0%

profile of v1, /device:TPU:19, one launch (start us, length us, event | category | flops | bytes accessed | tf_op | source)
XLA Modules:
  0.0 236.0 jit_solution(50471274355403419)
XLA Ops:
  4.3 1.9 collective-permute-start
  8.0 5.9 %collective-permute-done.1 = bf16[2,32,3584]{2,1,0:T(8,128)(2,1)S(1)} collective-permute-done((bf16[2,32,3584]{2,1,0:T(8,128)(2,1)S(1)}, bf16[2,32,3584]{2,1,0:T(8,128)(2,1)S(1)}, u32[]{:S(2)}, u32[]{:S(2)}) %collective-permute-start.1) | collective-permute-done | bytes 458784 | tf_op jit(solution)/shard_map/ppermute | solution.py:41
  13.9 4.4 %collective-permute-start.9 = (bf16[2,32,3584]{2,1,0:T(8,128)(2,1)S(1)}, bf16[2,32,3584]{2,1,0:T(8,128)(2,1)S(1)}, u32[]{:S(2)}, u32[]{:S(2)}) collective-permute-start(bf16[2,32,3584]{2,1,0:T(8,128)(2,1)S(1)} %get-tuple-element.6), channel_id=1, source_target_pairs={{0,9},{1,8},{2,11},{3,10},{4,13},{5,12},{6,15},{7,14},{8,17},{9,16... | collective-permute-start | bytes 1376264 | tf_op jit(solution)/shard_map/ppermute | solution.py:41
  18.4 10.2 %collective-permute-done.9 = bf16[2,32,3584]{2,1,0:T(8,128)(2,1)S(1)} collective-permute-done((bf16[2,32,3584]{2,1,0:T(8,128)(2,1)S(1)}, bf16[2,32,3584]{2,1,0:T(8,128)(2,1)S(1)}, u32[]{:S(2)}, u32[]{:S(2)}) %collective-permute-start.9) | collective-permute-done | bytes 458784 | tf_op jit(solution)/shard_map/ppermute | solution.py:41
  28.6 2.8 %collective-permute-start.16 = (bf16[2,32,3584]{2,1,0:T(8,128)(2,1)S(1)}, bf16[2,32,3584]{2,1,0:T(8,128)(2,1)S(1)}, u32[]{:S(2)}, u32[]{:S(2)}) collective-permute-start(bf16[2,32,3584]{2,1,0:T(8,128)(2,1)S(1)} %get-tuple-element.8), channel_id=1, source_target_pairs={{0,17},{1,16},{2,19},{3,18},{4,21},{5,20},{6,23},{7,22},{8,25},{9,... | collective-permute-start | bytes 1376264 | tf_op jit(solution)/shard_map/ppermute | solution.py:41
  31.4 22.7 %collective-permute-done.8 = bf16[2,32,3584]{2,1,0:T(8,128)(2,1)S(1)} collective-permute-done((bf16[2,32,3584]{2,1,0:T(8,128)(2,1)S(1)}, bf16[2,32,3584]{2,1,0:T(8,128)(2,1)S(1)}, u32[]{:S(2)}, u32[]{:S(2)}) %collective-permute-start.8) | collective-permute-done | bytes 458784 | tf_op jit(solution)/shard_map/ppermute | solution.py:41
  54.2 13.4 %collective-permute-done.16 = bf16[2,32,3584]{2,1,0:T(8,128)(2,1)S(1)} collective-permute-done((bf16[2,32,3584]{2,1,0:T(8,128)(2,1)S(1)}, bf16[2,32,3584]{2,1,0:T(8,128)(2,1)S(1)}, u32[]{:S(2)}, u32[]{:S(2)}) %collective-permute-start.16) | collective-permute-done | bytes 458784 | tf_op jit(solution)/shard_map/ppermute | solution.py:41
  67.6 9.8 %collective-permute-done.15 = bf16[2,32,3584]{2,1,0:T(8,128)(2,1)S(1)} collective-permute-done((bf16[2,32,3584]{2,1,0:T(8,128)(2,1)S(1)}, bf16[2,32,3584]{2,1,0:T(8,128)(2,1)S(1)}, u32[]{:S(2)}, u32[]{:S(2)}) %collective-permute-start.15) | collective-permute-done | bytes 458784 | tf_op jit(solution)/shard_map/ppermute | solution.py:41
  77.4 9.3 %collective-permute-start.22 = (bf16[2,32,3584]{2,1,0:T(8,128)(2,1)S(1)}, bf16[2,32,3584]{2,1,0:T(8,128)(2,1)S(1)}, u32[]{:S(2)}, u32[]{:S(2)}) collective-permute-start(bf16[2,32,3584]{2,1,0:T(8,128)(2,1)S(1)} %get-tuple-element.2), channel_id=1, source_target_pairs={{0,24},{1,25},{2,26},{3,27},{4,28},{5,29},{6,30},{7,31},{8,0},{9,1... | collective-permute-start | bytes 1376264 | tf_op jit(solution)/shard_map/ppermute | solution.py:41
  87.5 11.7 %collective-permute-done.22 = bf16[2,32,3584]{2,1,0:T(8,128)(2,1)S(1)} collective-permute-done((bf16[2,32,3584]{2,1,0:T(8,128)(2,1)S(1)}, bf16[2,32,3584]{2,1,0:T(8,128)(2,1)S(1)}, u32[]{:S(2)}, u32[]{:S(2)}) %collective-permute-start.22) | collective-permute-done | bytes 458784 | tf_op jit(solution)/shard_map/ppermute | solution.py:41
  100.8 6.0 %collective-permute-done.11 = bf16[2,32,3584]{2,1,0:T(8,128)(2,1)S(1)} collective-permute-done((bf16[2,32,3584]{2,1,0:T(8,128)(2,1)S(1)}, bf16[2,32,3584]{2,1,0:T(8,128)(2,1)S(1)}, u32[]{:S(2)}, u32[]{:S(2)}) %collective-permute-start.11) | collective-permute-done | bytes 458784 | tf_op jit(solution)/shard_map/ppermute | solution.py:41
  107.1 4.6 %collective-permute-done.10 = bf16[2,32,3584]{2,1,0:T(8,128)(2,1)S(1)} collective-permute-done((bf16[2,32,3584]{2,1,0:T(8,128)(2,1)S(1)}, bf16[2,32,3584]{2,1,0:T(8,128)(2,1)S(1)}, u32[]{:S(2)}, u32[]{:S(2)}) %collective-permute-start.10) | collective-permute-done | bytes 458784 | tf_op jit(solution)/shard_map/ppermute | solution.py:41
  112.0 4.6 %collective-permute-done.18 = bf16[2,32,3584]{2,1,0:T(8,128)(2,1)S(1)} collective-permute-done((bf16[2,32,3584]{2,1,0:T(8,128)(2,1)S(1)}, bf16[2,32,3584]{2,1,0:T(8,128)(2,1)S(1)}, u32[]{:S(2)}, u32[]{:S(2)}) %collective-permute-start.18) | collective-permute-done | bytes 458784 | tf_op jit(solution)/shard_map/ppermute | solution.py:41
  117.0 4.6 %collective-permute-done.17 = bf16[2,32,3584]{2,1,0:T(8,128)(2,1)S(1)} collective-permute-done((bf16[2,32,3584]{2,1,0:T(8,128)(2,1)S(1)}, bf16[2,32,3584]{2,1,0:T(8,128)(2,1)S(1)}, u32[]{:S(2)}, u32[]{:S(2)}) %collective-permute-start.17) | collective-permute-done | bytes 458784 | tf_op jit(solution)/shard_map/ppermute | solution.py:41
  121.9 4.6 %collective-permute-done.25 = bf16[2,32,3584]{2,1,0:T(8,128)(2,1)S(1)} collective-permute-done((bf16[2,32,3584]{2,1,0:T(8,128)(2,1)S(1)}, bf16[2,32,3584]{2,1,0:T(8,128)(2,1)S(1)}, u32[]{:S(2)}, u32[]{:S(2)}) %collective-permute-start.25) | collective-permute-done | bytes 458784 | tf_op jit(solution)/shard_map/ppermute | solution.py:41
  126.5 4.9 %collective-permute-done.24 = bf16[2,32,3584]{2,1,0:T(8,128)(2,1)S(1)} collective-permute-done((bf16[2,32,3584]{2,1,0:T(8,128)(2,1)S(1)}, bf16[2,32,3584]{2,1,0:T(8,128)(2,1)S(1)}, u32[]{:S(2)}, u32[]{:S(2)}) %collective-permute-start.24) | collective-permute-done | bytes 458784 | tf_op jit(solution)/shard_map/ppermute | solution.py:41
  153.5 1.4 multiply_reduce_fusion
  164.7 6.1 %collective-permute-start.30 = (f32[32]{0:T(128)S(1)}, f32[32]{0:T(128)S(1)}, u32[]{:S(2)}, u32[]{:S(2)}) collective-permute-start(f32[32]{0:T(128)S(1)} %get-tuple-element.54), channel_id=1, source_target_pairs={{0,1},{1,0},{2,3},{3,2},{4,5},{5,4},{6,7},{7,6},{8,9},{9,8},{10,11... | collective-permute-start | bytes 392 | tf_op jit(solution)/shard_map/ppermute | solution.py:41
  171.6 1.5 collective-permute-start.33
  173.1 2.3 collective-permute-done.32
  175.4 2.1 collective-permute-start.35
  177.5 2.3 collective-permute-start.36
  179.8 2.6 %collective-permute-start.38 = (f32[32]{0:T(128)S(1)}, f32[32]{0:T(128)S(1)}, u32[]{:S(2)}, u32[]{:S(2)}) collective-permute-start(f32[32]{0:T(128)S(1)} %get-tuple-element.49), channel_id=1, source_target_pairs={{0,8},{1,9},{2,10},{3,11},{4,12},{5,13},{6,14},{7,15},{8,16},{9,17... | collective-permute-start | bytes 392 | tf_op jit(solution)/shard_map/ppermute | solution.py:41
  182.3 1.8 collective-permute-start.39
  184.4 1.9 collective-permute-done.39
  187.1 1.7 collective-permute-start.7
  190.5 2.9 %collective-permute-start.14 = (bf16[32,3584]{1,0:T(8,128)(2,1)S(1)}, bf16[32,3584]{1,0:T(8,128)(2,1)S(1)}, u32[]{:S(2)}, u32[]{:S(2)}) collective-permute-start(bf16[32,3584]{1,0:T(8,128)(2,1)S(1)} %get-tuple-element.30), channel_id=1, source_target_pairs={{0,25},{1,24},{2,27},{3,26},{4,29},{5,28},{6,31},{7,30},{8,1},{9,0... | collective-permute-start | bytes 688136 | tf_op jit(solution)/shard_map/ppermute | solution.py:41
  198.8 4.2 %collective-permute-start.28 = (bf16[32,3584]{1,0:T(8,128)(2,1)S(1)}, bf16[32,3584]{1,0:T(8,128)(2,1)S(1)}, u32[]{:S(2)}, u32[]{:S(2)}) collective-permute-start(bf16[32,3584]{1,0:T(8,128)(2,1)S(1)} %get-tuple-element.10), channel_id=1, source_target_pairs={{0,9},{1,8},{2,11},{3,10},{4,13},{5,12},{6,15},{7,14},{8,17},{9,16... | collective-permute-start | bytes 688136 | tf_op jit(solution)/shard_map/ppermute | solution.py:41
  203.5 20.7 %collective-permute-done.20 = bf16[32,3584]{1,0:T(8,128)(2,1)S(1)} collective-permute-done((bf16[32,3584]{1,0:T(8,128)(2,1)S(1)}, bf16[32,3584]{1,0:T(8,128)(2,1)S(1)}, u32[]{:S(2)}, u32[]{:S(2)}) %collective-permute-start.20) | collective-permute-done | bytes 229408 | tf_op jit(solution)/shard_map/ppermute | solution.py:41
  224.2 4.9 %collective-permute-done.21 = bf16[32,3584]{1,0:T(8,128)(2,1)S(1)} collective-permute-done((bf16[32,3584]{1,0:T(8,128)(2,1)S(1)}, bf16[32,3584]{1,0:T(8,128)(2,1)S(1)}, u32[]{:S(2)}, u32[]{:S(2)}) %collective-permute-start.21) | collective-permute-done | bytes 229408 | tf_op jit(solution)/shard_map/ppermute | solution.py:41
  229.7 4.9 %collective-permute-done.28 = bf16[32,3584]{1,0:T(8,128)(2,1)S(1)} collective-permute-done((bf16[32,3584]{1,0:T(8,128)(2,1)S(1)}, bf16[32,3584]{1,0:T(8,128)(2,1)S(1)}, u32[]{:S(2)}, u32[]{:S(2)}) %collective-permute-start.28) | collective-permute-done | bytes 229408 | tf_op jit(solution)/shard_map/ppermute | solution.py:41
  234.6 1.4 fusion
  (148 shorter events, 50.9 us)
Async XLA Ops:
  4.0 9.9 %collective-permute-start.1 = (bf16[2,32,3584]{2,1,0:T(8,128)(2,1)S(1)}, bf16[2,32,3584]{2,1,0:T(8,128)(2,1)S(1)}, u32[]{:S(2)}, u32[]{:S(2)}) collective-permute-start(bf16[2,32,3584]{2,1,0:T(8,128)(2,1)S(1)} %get-tuple-element.4), channel_id=1, source_target_pairs={{0,4},{1,3},{2,6},{3,1},{4,0},{5,7},{6,2},{7,5},{8,12},{9,11},{10,... | collective-permute-start | bytes 1376264 | tf_op jit(solution)/shard_map/ppermute | solution.py:41
  4.3 14.0 %collective-permute-start = (bf16[2,32,3584]{2,1,0:T(8,128)(2,1)S(1)}, bf16[2,32,3584]{2,1,0:T(8,128)(2,1)S(1)}, u32[]{:S(2)}, u32[]{:S(2)}) collective-permute-start(bf16[2,32,3584]{2,1,0:T(8,128)(2,1)S(1)} %get-tuple-element.3), channel_id=1, source_target_pairs={{0,1},{1,0},{2,3},{3,2},{4,5},{5,4},{6,7},{7,6},{8,9},{9,8},{10,11... | collective-permute-start | bytes 1376264 | tf_op jit(solution)/shard_map/ppermute | solution.py:41
  6.3 125.2 %collective-permute-start.4 = (bf16[3584,256]{1,0:T(8,128)(2,1)S(1)}, bf16[3584,256]{1,0:T(8,128)(2,1)S(1)}, u32[]{:S(2)}, u32[]{:S(2)}) collective-permute-start(bf16[3584,256]{1,0:T(8,128)(2,1)S(1)} %bitcast.93), channel_id=1, source_target_pairs={{0,2},{1,5},{2,0},{3,7},{4,6},{5,1},{6,4},{7,3},{8,10},{9,13},{10,... | collective-permute-start | bytes 5505032 | tf_op jit(solution)/shard_map/ppermute | solution.py:41
  6.5 125.6 %collective-permute-start.5 = (bf16[3584,256]{1,0:T(8,128)(2,1)S(1)}, bf16[3584,256]{1,0:T(8,128)(2,1)S(1)}, u32[]{:S(2)}, u32[]{:S(2)}) collective-permute-start(bf16[3584,256]{1,0:T(8,128)(2,1)S(1)} %bitcast.102), channel_id=1, source_target_pairs={{0,2},{1,5},{2,0},{3,7},{4,6},{5,1},{6,4},{7,3},{8,10},{9,13},{10,... | collective-permute-start | bytes 5505032 | tf_op jit(solution)/shard_map/ppermute | solution.py:41
  7.7 125.0 %collective-permute-start.3 = (bf16[256,3584]{1,0:T(8,128)(2,1)S(1)}, bf16[256,3584]{1,0:T(8,128)(2,1)S(1)}, u32[]{:S(2)}, u32[]{:S(2)}) collective-permute-start(bf16[256,3584]{1,0:T(8,128)(2,1)S(1)} %bitcast.88), channel_id=1, source_target_pairs={{0,2},{1,5},{2,0},{3,7},{4,6},{5,1},{6,4},{7,3},{8,10},{9,13},{10,... | collective-permute-start | bytes 5505032 | tf_op jit(solution)/shard_map/ppermute | solution.py:41
  13.9 14.8 %collective-permute-start.9 = (bf16[2,32,3584]{2,1,0:T(8,128)(2,1)S(1)}, bf16[2,32,3584]{2,1,0:T(8,128)(2,1)S(1)}, u32[]{:S(2)}, u32[]{:S(2)}) collective-permute-start(bf16[2,32,3584]{2,1,0:T(8,128)(2,1)S(1)} %get-tuple-element.6), channel_id=1, source_target_pairs={{0,9},{1,8},{2,11},{3,10},{4,13},{5,12},{6,15},{7,14},{8,17},{9,16... | collective-permute-start | bytes 1376264 | tf_op jit(solution)/shard_map/ppermute | solution.py:41
  18.3 35.8 %collective-permute-start.8 = (bf16[2,32,3584]{2,1,0:T(8,128)(2,1)S(1)}, bf16[2,32,3584]{2,1,0:T(8,128)(2,1)S(1)}, u32[]{:S(2)}, u32[]{:S(2)}) collective-permute-start(bf16[2,32,3584]{2,1,0:T(8,128)(2,1)S(1)} %get-tuple-element.5), channel_id=1, source_target_pairs={{0,8},{1,9},{2,10},{3,11},{4,12},{5,13},{6,14},{7,15},{8,16},{9,17... | collective-permute-start | bytes 1376264 | tf_op jit(solution)/shard_map/ppermute | solution.py:41
  28.6 38.9 %collective-permute-start.16 = (bf16[2,32,3584]{2,1,0:T(8,128)(2,1)S(1)}, bf16[2,32,3584]{2,1,0:T(8,128)(2,1)S(1)}, u32[]{:S(2)}, u32[]{:S(2)}) collective-permute-start(bf16[2,32,3584]{2,1,0:T(8,128)(2,1)S(1)} %get-tuple-element.8), channel_id=1, source_target_pairs={{0,17},{1,16},{2,19},{3,18},{4,21},{5,20},{6,23},{7,22},{8,25},{9,... | collective-permute-start | bytes 1376264 | tf_op jit(solution)/shard_map/ppermute | solution.py:41
  54.1 23.3 %collective-permute-start.15 = (bf16[2,32,3584]{2,1,0:T(8,128)(2,1)S(1)}, bf16[2,32,3584]{2,1,0:T(8,128)(2,1)S(1)}, u32[]{:S(2)}, u32[]{:S(2)}) collective-permute-start(bf16[2,32,3584]{2,1,0:T(8,128)(2,1)S(1)} %get-tuple-element.7), channel_id=1, source_target_pairs={{0,16},{1,17},{2,18},{3,19},{4,20},{5,21},{6,22},{7,23},{8,24},{9,... | collective-permute-start | bytes 1376264 | tf_op jit(solution)/shard_map/ppermute | solution.py:41
  67.6 19.7 %collective-permute-start.23 = (bf16[2,32,3584]{2,1,0:T(8,128)(2,1)S(1)}, bf16[2,32,3584]{2,1,0:T(8,128)(2,1)S(1)}, u32[]{:S(2)}, u32[]{:S(2)}) collective-permute-start(bf16[2,32,3584]{2,1,0:T(8,128)(2,1)S(1)} %get-tuple-element.9), channel_id=1, source_target_pairs={{0,25},{1,24},{2,27},{3,26},{4,29},{5,28},{6,31},{7,30},{8,1},{9,0... | collective-permute-start | bytes 1376264 | tf_op jit(solution)/shard_map/ppermute | solution.py:41
  77.4 21.8 %collective-permute-start.22 = (bf16[2,32,3584]{2,1,0:T(8,128)(2,1)S(1)}, bf16[2,32,3584]{2,1,0:T(8,128)(2,1)S(1)}, u32[]{:S(2)}, u32[]{:S(2)}) collective-permute-start(bf16[2,32,3584]{2,1,0:T(8,128)(2,1)S(1)} %get-tuple-element.2), channel_id=1, source_target_pairs={{0,24},{1,25},{2,26},{3,27},{4,28},{5,29},{6,30},{7,31},{8,0},{9,1... | collective-permute-start | bytes 1376264 | tf_op jit(solution)/shard_map/ppermute | solution.py:41
  87.3 12.2 %collective-permute-start.2 = (bf16[2,32,3584]{2,1,0:T(8,128)(2,1)S(1)}, bf16[2,32,3584]{2,1,0:T(8,128)(2,1)S(1)}, u32[]{:S(2)}, u32[]{:S(2)}) collective-permute-start(bf16[2,32,3584]{2,1,0:T(8,128)(2,1)S(1)} %collective-permute-done), channel_id=1, source_target_pairs={{0,4},{1,3},{2,6},{3,1},{4,0},{5,7},{6,2},{7,5},{8,12},{9,11},{10,... | collective-permute-start | bytes 1376264 | tf_op jit(solution)/shard_map/ppermute | solution.py:41
  99.2 7.6 %collective-permute-start.11 = (bf16[2,32,3584]{2,1,0:T(8,128)(2,1)S(1)}, bf16[2,32,3584]{2,1,0:T(8,128)(2,1)S(1)}, u32[]{:S(2)}, u32[]{:S(2)}) collective-permute-start(bf16[2,32,3584]{2,1,0:T(8,128)(2,1)S(1)} %collective-permute-done.9), channel_id=1, source_target_pairs={{0,4},{1,3},{2,6},{3,1},{4,0},{5,7},{6,2},{7,5},{8,12},{9,11},{10,... | collective-permute-start | bytes 1376264 | tf_op jit(solution)/shard_map/ppermute | solution.py:41
  99.5 12.2 %collective-permute-start.10 = (bf16[2,32,3584]{2,1,0:T(8,128)(2,1)S(1)}, bf16[2,32,3584]{2,1,0:T(8,128)(2,1)S(1)}, u32[]{:S(2)}, u32[]{:S(2)}) collective-permute-start(bf16[2,32,3584]{2,1,0:T(8,128)(2,1)S(1)} %collective-permute-done.8), channel_id=1, source_target_pairs={{0,4},{1,3},{2,6},{3,1},{4,0},{5,7},{6,2},{7,5},{8,12},{9,11},{10,... | collective-permute-start | bytes 1376264 | tf_op jit(solution)/shard_map/ppermute | solution.py:41
  106.8 9.8 %collective-permute-start.18 = (bf16[2,32,3584]{2,1,0:T(8,128)(2,1)S(1)}, bf16[2,32,3584]{2,1,0:T(8,128)(2,1)S(1)}, u32[]{:S(2)}, u32[]{:S(2)}) collective-permute-start(bf16[2,32,3584]{2,1,0:T(8,128)(2,1)S(1)} %collective-permute-done.16), channel_id=1, source_target_pairs={{0,4},{1,3},{2,6},{3,1},{4,0},{5,7},{6,2},{7,5},{8,12},{9,11},{10,... | collective-permute-start | bytes 1376264 | tf_op jit(solution)/shard_map/ppermute | solution.py:41
  111.7 9.8 %collective-permute-start.17 = (bf16[2,32,3584]{2,1,0:T(8,128)(2,1)S(1)}, bf16[2,32,3584]{2,1,0:T(8,128)(2,1)S(1)}, u32[]{:S(2)}, u32[]{:S(2)}) collective-permute-start(bf16[2,32,3584]{2,1,0:T(8,128)(2,1)S(1)} %collective-permute-done.15), channel_id=1, source_target_pairs={{0,4},{1,3},{2,6},{3,1},{4,0},{5,7},{6,2},{7,5},{8,12},{9,11},{10,... | collective-permute-start | bytes 1376264 | tf_op jit(solution)/shard_map/ppermute | solution.py:41
  116.7 9.8 %collective-permute-start.25 = (bf16[2,32,3584]{2,1,0:T(8,128)(2,1)S(1)}, bf16[2,32,3584]{2,1,0:T(8,128)(2,1)S(1)}, u32[]{:S(2)}, u32[]{:S(2)}) collective-permute-start(bf16[2,32,3584]{2,1,0:T(8,128)(2,1)S(1)} %collective-permute-done.23), channel_id=1, source_target_pairs={{0,4},{1,3},{2,6},{3,1},{4,0},{5,7},{6,2},{7,5},{8,12},{9,11},{10,... | collective-permute-start | bytes 1376264 | tf_op jit(solution)/shard_map/ppermute | solution.py:41
  121.6 9.8 %collective-permute-start.24 = (bf16[2,32,3584]{2,1,0:T(8,128)(2,1)S(1)}, bf16[2,32,3584]{2,1,0:T(8,128)(2,1)S(1)}, u32[]{:S(2)}, u32[]{:S(2)}) collective-permute-start(bf16[2,32,3584]{2,1,0:T(8,128)(2,1)S(1)} %collective-permute-done.22), channel_id=1, source_target_pairs={{0,4},{1,3},{2,6},{3,1},{4,0},{5,7},{6,2},{7,5},{8,12},{9,11},{10,... | collective-permute-start | bytes 1376264 | tf_op jit(solution)/shard_map/ppermute | solution.py:41
  137.6 49.3 %collective-permute-start.6 = (bf16[64,3584]{1,0:T(8,128)(2,1)}, bf16[64,3584]{1,0:T(8,128)(2,1)S(1)}, u32[]{:S(2)}, u32[]{:S(2)}) collective-permute-start(bf16[64,3584]{1,0:T(8,128)(2,1)} %slice.486), channel_id=1, source_target_pairs={{0,4},{1,3},{2,6},{3,1},{4,0},{5,7},{6,2},{7,5},{8,12},{9,11},{10,... | collective-permute-start | bytes 1376264 | tf_op jit(solution)/shard_map/ppermute | solution.py:41
  144.1 44.6 %collective-permute-start.12 = (bf16[64,3584]{1,0:T(8,128)(2,1)}, bf16[64,3584]{1,0:T(8,128)(2,1)}, u32[]{:S(2)}, u32[]{:S(2)}) collective-permute-start(bf16[64,3584]{1,0:T(8,128)(2,1)} %slice.485), channel_id=1, source_target_pairs={{0,4},{1,3},{2,6},{3,1},{4,0},{5,7},{6,2},{7,5},{8,12},{9,11},{10,... | collective-permute-start | bytes 1376264 | tf_op jit(solution)/shard_map/ppermute | solution.py:41
  151.7 41.7 %collective-permute-start.19 = (bf16[64,3584]{1,0:T(8,128)(2,1)}, bf16[64,3584]{1,0:T(8,128)(2,1)}, u32[]{:S(2)}, u32[]{:S(2)}) collective-permute-start(bf16[64,3584]{1,0:T(8,128)(2,1)} %slice.484), channel_id=1, source_target_pairs={{0,4},{1,3},{2,6},{3,1},{4,0},{5,7},{6,2},{7,5},{8,12},{9,11},{10,... | collective-permute-start | bytes 1376264 | tf_op jit(solution)/shard_map/ppermute | solution.py:41
  163.4 7.5 %collective-permute-start.37 = (f32[64]{0:T(128)S(1)}, f32[64]{0:T(128)S(1)}, u32[]{:S(2)}, u32[]{:S(2)}) collective-permute-start(f32[64]{0:T(128)S(1)} %slice.297), channel_id=1, source_target_pairs={{0,4},{1,3},{2,6},{3,1},{4,0},{5,7},{6,2},{7,5},{8,12},{9,11},{10,... | collective-permute-start | bytes 776 | tf_op jit(solution)/shard_map/ppermute | solution.py:41
  164.7 6.9 %collective-permute-start.30 = (f32[32]{0:T(128)S(1)}, f32[32]{0:T(128)S(1)}, u32[]{:S(2)}, u32[]{:S(2)}) collective-permute-start(f32[32]{0:T(128)S(1)} %get-tuple-element.54), channel_id=1, source_target_pairs={{0,1},{1,0},{2,3},{3,2},{4,5},{5,4},{6,7},{7,6},{8,9},{9,8},{10,11... | collective-permute-start | bytes 392 | tf_op jit(solution)/shard_map/ppermute | solution.py:41
  171.6 5.8 %collective-permute-start.33 = (f32[32]{0:T(128)S(1)}, f32[32]{0:T(128)S(1)}, u32[]{:S(2)}, u32[]{:S(2)}) collective-permute-start(f32[32]{0:T(128)S(1)} %get-tuple-element.52), channel_id=1, source_target_pairs={{0,25},{1,24},{2,27},{3,26},{4,29},{5,28},{6,31},{7,30},{8,1},{9,0... | collective-permute-start | bytes 392 | tf_op jit(solution)/shard_map/ppermute | solution.py:41
  184.2 11.7 %collective-permute-start.26 = (bf16[64,3584]{1,0:T(8,128)(2,1)}, bf16[64,3584]{1,0:T(8,128)(2,1)}, u32[]{:S(2)}, u32[]{:S(2)}) collective-permute-start(bf16[64,3584]{1,0:T(8,128)(2,1)} %slice.483), channel_id=1, source_target_pairs={{0,4},{1,3},{2,6},{3,1},{4,0},{5,7},{6,2},{7,5},{8,12},{9,11},{10,... | collective-permute-start | bytes 1376264 | tf_op jit(solution)/shard_map/ppermute | solution.py:41
  187.1 10.9 %collective-permute-start.7 = (bf16[32,3584]{1,0:T(8,128)(2,1)S(1)}, bf16[32,3584]{1,0:T(8,128)(2,1)S(1)}, u32[]{:S(2)}, u32[]{:S(2)}) collective-permute-start(bf16[32,3584]{1,0:T(8,128)(2,1)S(1)} %get-tuple-element.40), channel_id=1, source_target_pairs={{0,1},{1,0},{2,3},{3,2},{4,5},{5,4},{6,7},{7,6},{8,9},{9,8},{10,11... | collective-permute-start | bytes 688136 | tf_op jit(solution)/shard_map/ppermute | solution.py:41
  189.9 8.9 %collective-permute-start.13 = (bf16[32,3584]{1,0:T(8,128)(2,1)S(1)}, bf16[32,3584]{1,0:T(8,128)(2,1)S(1)}, u32[]{:S(2)}, u32[]{:S(2)}) collective-permute-start(bf16[32,3584]{1,0:T(8,128)(2,1)S(1)} %get-tuple-element.31), channel_id=1, source_target_pairs={{0,24},{1,25},{2,26},{3,27},{4,28},{5,29},{6,30},{7,31},{8,0},{9,1... | collective-permute-start | bytes 688136 | tf_op jit(solution)/shard_map/ppermute | solution.py:41
  190.5 13.1 %collective-permute-start.14 = (bf16[32,3584]{1,0:T(8,128)(2,1)S(1)}, bf16[32,3584]{1,0:T(8,128)(2,1)S(1)}, u32[]{:S(2)}, u32[]{:S(2)}) collective-permute-start(bf16[32,3584]{1,0:T(8,128)(2,1)S(1)} %get-tuple-element.30), channel_id=1, source_target_pairs={{0,25},{1,24},{2,27},{3,26},{4,29},{5,28},{6,31},{7,30},{8,1},{9,0... | collective-permute-start | bytes 688136 | tf_op jit(solution)/shard_map/ppermute | solution.py:41
  194.5 29.7 %collective-permute-start.20 = (bf16[32,3584]{1,0:T(8,128)(2,1)S(1)}, bf16[32,3584]{1,0:T(8,128)(2,1)S(1)}, u32[]{:S(2)}, u32[]{:S(2)}) collective-permute-start(bf16[32,3584]{1,0:T(8,128)(2,1)S(1)} %get-tuple-element.21), channel_id=1, source_target_pairs={{0,16},{1,17},{2,18},{3,19},{4,20},{5,21},{6,22},{7,23},{8,24},{9,... | collective-permute-start | bytes 688136 | tf_op jit(solution)/shard_map/ppermute | solution.py:41
  195.8 33.3 %collective-permute-start.21 = (bf16[32,3584]{1,0:T(8,128)(2,1)S(1)}, bf16[32,3584]{1,0:T(8,128)(2,1)S(1)}, u32[]{:S(2)}, u32[]{:S(2)}) collective-permute-start(bf16[32,3584]{1,0:T(8,128)(2,1)S(1)} %get-tuple-element.20), channel_id=1, source_target_pairs={{0,17},{1,16},{2,19},{3,18},{4,21},{5,20},{6,23},{7,22},{8,25},{9,... | collective-permute-start | bytes 688136 | tf_op jit(solution)/shard_map/ppermute | solution.py:41
  198.0 31.7 %collective-permute-start.27 = (bf16[32,3584]{1,0:T(8,128)(2,1)S(1)}, bf16[32,3584]{1,0:T(8,128)(2,1)S(1)}, u32[]{:S(2)}, u32[]{:S(2)}) collective-permute-start(bf16[32,3584]{1,0:T(8,128)(2,1)S(1)} %get-tuple-element.11), channel_id=1, source_target_pairs={{0,8},{1,9},{2,10},{3,11},{4,12},{5,13},{6,14},{7,15},{8,16},{9,17... | collective-permute-start | bytes 688136 | tf_op jit(solution)/shard_map/ppermute | solution.py:41
  198.8 35.8 %collective-permute-start.28 = (bf16[32,3584]{1,0:T(8,128)(2,1)S(1)}, bf16[32,3584]{1,0:T(8,128)(2,1)S(1)}, u32[]{:S(2)}, u32[]{:S(2)}) collective-permute-start(bf16[32,3584]{1,0:T(8,128)(2,1)S(1)} %get-tuple-element.10), channel_id=1, source_target_pairs={{0,9},{1,8},{2,11},{3,10},{4,13},{5,12},{6,15},{7,14},{8,17},{9,16... | collective-permute-start | bytes 688136 | tf_op jit(solution)/shard_map/ppermute | solution.py:41
  (20 other events, 101.5 us)

commit v2 on v1

v2 whole, which is shorter than its diff:
```python
import jax
import jax.numpy as jnp
from jax import lax
from jax.sharding import PartitionSpec as P

SHARDS = 4
LANES = 128
AXES = ("wide", "narrow")


def silu_parts(gate):
    sigma = jax.nn.sigmoid(gate)
    return (gate * sigma, sigma * (1.0 + gate * (1.0 - sigma)))


def times(left, right):
    return jnp.dot(left, right, preferred_element_type=jnp.float32)


def times_transposed(left, right):
    return lax.dot_general(
        left, right, (((1,), (1,)), ((), ())), preferred_element_type=jnp.float32
    )


def tie(value, *before):
    return lax.optimization_barrier((value,) + before)[0]


def with_prob(rows, prob):
    high = lax.reduce_precision(prob, 8, 7)
    column = lax.broadcasted_iota(jnp.int32, (prob.shape[0], LANES), 1)
    tail = jnp.where(
        column == 0, high[:, None], jnp.where(column == 1, (prob - high)[:, None], 0.0)
    )
    return jnp.concatenate([rows.astype(jnp.bfloat16), tail.astype(jnp.bfloat16)], axis=1)


def shards(tokens, grad_out, expert_ids, combine, w_gate, w_up, w_down):
    wide = lax.axis_size("wide")
    narrow = lax.axis_size("narrow")
    blocks = wide // SHARDS
    experts = blocks * narrow
    count, width = tokens.shape
    cap = 2 * count // experts
    half = narrow * cap
    block = lax.axis_index("wide") // SHARDS
    core = lax.axis_index("narrow")

    def permute(value, target):
        pairs = []
        for w in range(wide):
            for c in range(narrow):
                b, s, n = target(w // SHARDS, w % SHARDS, c)
                pairs.append((w * narrow + c, (b * SHARDS + s) * narrow + n))
        return lax.ppermute(value, AXES, pairs)

    def swap_weights(value):
        return permute(value, lambda b, s, c: (b, s ^ (1 if c == 0 else 2), c))

    def swap_rows(value):
        return permute(value, lambda b, s, c: (b, s ^ (2 if c == 0 else 1), c))

    def send(value, k, m):
        return permute(value, lambda b, s, c: (b ^ k, s, (c + m) % narrow))

    def give_back(value, k, m):
        if k == 0 and m == 0:
            return value
        return permute(value, lambda b, s, c: (b ^ k, s, (c - m) % narrow))

    both_w = jnp.concatenate([w_gate[0], w_up[0]], axis=1)
    both_in = swap_weights(both_w)
    down_in = swap_weights(w_down[0])
    units = w_gate.shape[2]

    order = [blocks // 2] + [k for k in range(1, blocks) if k != blocks // 2] + [0]
    token = jnp.arange(count, dtype=jnp.int32)
    twins = (expert_ids[:, None] == expert_ids[None, :]) & (token[:, None] < token[None, :])
    slot = jnp.sum(twins.astype(jnp.int32), axis=0)
    shift = (expert_ids % blocks) ^ block
    position = sum(i * (shift == k).astype(jnp.int32) for i, k in enumerate(order))
    turn = (expert_ids // blocks - core + narrow) % narrow
    place = (position * narrow + turn) * cap + slot
    select = jnp.arange(experts * cap, dtype=jnp.int32)[:, None] == place[None, :]
    packed_x = times(select.astype(jnp.bfloat16), tokens).astype(jnp.bfloat16)
    packed_g = times(select.astype(jnp.bfloat16), grad_out).astype(jnp.bfloat16)
    packed = jnp.stack(
        [
            packed_x.reshape(blocks, narrow, cap, width),
            packed_g.reshape(blocks, narrow, cap, width),
        ],
        axis=2,
    )

    turned = [
        permute(packed[:, m], lambda b, s, c: (b, s, (c + m) % narrow)) for m in range(1, narrow)
    ]
    merged = jnp.stack([packed[:, 0]] + turned, axis=1)
    arrived = []
    for i, k in enumerate(order):
        if k == 0:
            arrived.append(merged[i])
        else:
            chunk = merged[i] if i < 2 else tie(merged[i], arrived[i - 2])
            arrived.append(send(chunk, k, 0))

    swapped = [None] * blocks

    def swap_in(i, *wait):
        swapped[i] = swap_rows(tie(arrived[i], *wait))

    def compute(i, *wait):
        mine, other = arrived[i], tie(swapped[i], *wait)
        x = jnp.concatenate([mine[:, 0].reshape(half, width), other[:, 0].reshape(half, width)])
        g = jnp.concatenate([mine[:, 1].reshape(half, width), other[:, 1].reshape(half, width)])
        partial, prob = 0.0, 0.0
        for forward_w, down_w in ((both_w, w_down[0]), (both_in, down_in)):
            forward = times(x, forward_w)
            gate, up = forward[:, :units], forward[:, units:]
            back = times_transposed(g, down_w)
            act, slope = silu_parts(gate)
            prob = prob + jnp.sum(act * up * back, axis=1)
            grads = jnp.concatenate([back * up * slope, back * act], axis=1).astype(jnp.bfloat16)
            partial = partial + times_transposed(grads, forward_w)
        theirs = with_prob(partial[half:], prob[half:])
        return partial[:half], prob[:half], theirs

    def finish(i, part, *wait):
        partial, prob, theirs = part
        theirs = tie(swap_rows(theirs), *wait).astype(jnp.float32)
        total = with_prob(
            partial + theirs[:, :width], prob + (theirs[:, width] + theirs[:, width + 1])
        )
        return total

    parts = [None] * blocks
    totals = [None] * blocks
    swap_in(0)
    swap_in(1)
    for first in range(0, blocks, 2):
        last = min(first + 1, blocks - 1)
        for i in range(first, last + 1):
            wait = [parts[i - 1][2]] if i > first else []
            if i == first and i > 0:
                wait.append(totals[i - 1])
            parts[i] = compute(i, *wait)
            if i == first:
                for j in range(last + 1, min(last + 3, blocks)):
                    swap_in(j, parts[i][2], arrived[min(last + 1, blocks - 1)])
        for i in range(first, last + 1):
            totals[i] = finish(i, parts[i], parts[last][2])

    rows = 0.0
    select = select.T.reshape(count, blocks, half).astype(jnp.bfloat16)
    for i in range(blocks):
        total = totals[i] if order[i] == 0 else give_back(totals[i], order[i], 0)
        parts_in = [total[:cap]]
        for m in range(1, narrow):
            parts_in.append(give_back(total[m * cap : (m + 1) * cap], 0, m))
        rows = rows + times(select[:, i], jnp.concatenate(parts_in, axis=0))
    token_grad = (combine[:, None] * rows[:, :width]).astype(jnp.bfloat16)
    prob_grad = rows[:, width] + rows[:, width + 1]
    return (token_grad, prob_grad)


def solution(mesh):
    in_specs = (
        P(("parts", "wide", "narrow"), None),
        P(("parts", "wide", "narrow"), None),
        P(("parts", "wide", "narrow")),
        P(("parts", "wide", "narrow")),
        P("narrow", None, "wide"),
        P("narrow", None, "wide"),
        P("narrow", "wide", None),
    )
    out_specs = (P(("parts", "wide", "narrow"), None), P(("parts", "wide", "narrow")))
    return jax.shard_map(shards, mesh=mesh, in_specs=in_specs, out_specs=out_specs, check_vma=False)
```

time: 236 us -> 164 us (0.69)
  waiting for transfers between devices: 141 us -> 105 us
  starting transfers between devices: 57 us -> 23.1 us
  local copies, waits for them, and re-layouts: 6.3 us -> 1.78 us
    ppermute x40 -> x21, waiting for transfers between devices: 141 us -> 105 us  [permute(): return lax.ppermute(value, AXES, pairs)]
    ppermute x40 -> x21, starting transfers between devices: 57 us -> 23.1 us  [permute(): return lax.ppermute(value, AXES, pairs)]
    slice x18 -> x15, local copies, waits for them, and re-layouts: 4.34 us -> 0.78 us  [the longest x4 0.24 us: compute(): mine[:, 0].reshape(half, width)]
    dot_general x12 -> x16, matrix products: 16.1 us -> 17 us  [times_transposed(): lax.dot_general(left, right, (((1,), (1,)), ((), ())), preferred_element_...]
    dot_general x11 -> x14, matrix products: 7.96 us -> 8.23 us  [times(): return jnp.dot(left, right, preferred_element_type=jnp.float32)]
  transfers between devices with their start and end apart: 40 -> 21, of which waited for: 23 -> 12; matrix products, arithmetic and copies ran while one was open for 11% -> 17% of each run, Pallas kernels for 0% -> 0%
where the time goes in v2:
time: 164 us
  waiting for transfers between devices  105 us (64%)
  matrix products  25.2 us (15%)
  starting transfers between devices  23.1 us (14%)
  other arithmetic  6.97 us (4%)
  local copies, waits for them, and re-layouts  1.78 us (1%)
    ppermute x21, waiting for transfers between devices, permute(): return lax.ppermute(value, AXES, pairs)  105 us
    ppermute x21, starting transfers between devices, permute(): return lax.ppermute(value, AXES, pairs)  23.1 us
    dot_general x16, matrix products, times_transposed(): lax.dot_general(left, right, (((1,), (1,)), ((), ())), preferred_element_...  17 us
    dot_general x14, matrix products, times(): return jnp.dot(left, right, preferred_element_type=jnp.float32)  8.23 us
  transfers between devices with their start and end apart: 21, of which 12 were waited for; matrix products, arithmetic and copies ran while one was open for 17% of the time, Pallas kernels for 0%

profile of v2, /device:TPU:19, one launch (start us, length us, event | category | flops | bytes accessed | tf_op | source)
XLA Modules:
  0.0 163.7 jit_solution(1954568131542257354)
XLA Ops:
  0.7 0.9 convert_reduce_fusion
  5.9 1.3 collective-permute-start.4
  7.2 1.1 collective-permute-start.3
  9.0 1.3 collective-permute-start.6
  10.3 37.7 %collective-permute-done.1 = bf16[2,2,32,3584]{3,2,1,0:T(8,128)(2,1)S(1)} collective-permute-done((bf16[2,2,32,3584]{3,2,1,0:T(8,128)(2,1)S(1)}, bf16[2,2,32,3584]{3,2,1,0:T(8,128)(2,1)S(1)}, u32[]{:S(2)}, u32[]{:S(2)}) %collective-permute-start.1) | collective-permute-done | bytes 917536 | tf_op jit(solution)/shard_map/ppermute | solution.py:56
  48.1 2.0 %collective-permute-done.6 = bf16[2,2,32,3584]{3,2,1,0:T(8,128)(2,1)S(1)} collective-permute-done((bf16[2,2,32,3584]{3,2,1,0:T(8,128)(2,1)S(1)}, bf16[2,2,32,3584]{3,2,1,0:T(8,128)(2,1)S(1)}, u32[]{:S(2)}, u32[]{:S(2)}) %collective-permute-start.6) | collective-permute-done | bytes 917536 | tf_op jit(solution)/shard_map/ppermute | solution.py:56
  50.1 2.4 %collective-permute-start.13 = (bf16[2,2,32,3584]{3,2,1,0:T(8,128)(2,1)S(1)}, bf16[2,2,32,3584]{3,2,1,0:T(8,128)(2,1)S(1)}, u32[]{:S(2)}, u32[]{:S(2)}) collective-permute-start(bf16[2,2,32,3584]{3,2,1,0:T(8,128)(2,1)S(1)} %get-tuple-element.15), channel_id=1, source_target_pairs={{0,24},{1,25},{2,26},{3,27},{4,28},{5,29},{6,30},{7,31},{8,16},{9,... | collective-permute-start | bytes 2752520 | tf_op jit(solution)/shard_map/ppermute | solution.py:56
  52.6 17.9 %collective-permute-done.2 = bf16[2,2,32,3584]{3,2,1,0:T(8,128)(2,1)S(1)} collective-permute-done((bf16[2,2,32,3584]{3,2,1,0:T(8,128)(2,1)S(1)}, bf16[2,2,32,3584]{3,2,1,0:T(8,128)(2,1)S(1)}, u32[]{:S(2)}, u32[]{:S(2)}) %collective-permute-start.2) | collective-permute-done | bytes 917536 | tf_op jit(solution)/shard_map/ppermute | solution.py:56
  72.0 1.3 fusion.49
  74.0 8.8 %collective-permute-done.3 = bf16[256,3584]{1,0:T(8,128)(2,1)S(1)} collective-permute-done((bf16[256,3584]{1,0:T(8,128)(2,1)S(1)}, bf16[256,3584]{1,0:T(8,128)(2,1)S(1)}, u32[]{:S(2)}, u32[]{:S(2)}) %collective-permute-start.3) | collective-permute-done | bytes 1835040 | tf_op jit(solution)/shard_map/ppermute | solution.py:56
  82.8 0.8 multiply_convert_fusion.13
  83.6 1.3 convolution_add_fusion.3
  85.5 2.9 %collective-permute-done.7 = bf16[2,2,32,3584]{3,2,1,0:T(8,128)(2,1)S(1)} collective-permute-done((bf16[2,2,32,3584]{3,2,1,0:T(8,128)(2,1)S(1)}, bf16[2,2,32,3584]{3,2,1,0:T(8,128)(2,1)S(1)}, u32[]{:S(2)}, u32[]{:S(2)}) %collective-permute-start.7) | collective-permute-done | bytes 917536 | tf_op jit(solution)/shard_map/ppermute | solution.py:56
  89.9 1.3 fusion.56
  92.7 1.3 convolution_add_fusion.2
  94.6 1.2 collective-permute-start.14
  96.5 5.6 %collective-permute-done.10 = bf16[64,3712]{1,0:T(8,128)(2,1)S(1)} collective-permute-done((bf16[64,3712]{1,0:T(8,128)(2,1)S(1)}, bf16[64,3712]{1,0:T(8,128)(2,1)S(1)}, u32[]{:S(2)}, u32[]{:S(2)}) %collective-permute-start.10) | collective-permute-done | bytes 475168 | tf_op jit(solution)/shard_map/ppermute | solution.py:56
  102.8 1.4 collective-permute-start.11
  104.2 7.8 %collective-permute-done.14 = bf16[2,2,32,3584]{3,2,1,0:T(8,128)(2,1)S(1)} collective-permute-done((bf16[2,2,32,3584]{3,2,1,0:T(8,128)(2,1)S(1)}, bf16[2,2,32,3584]{3,2,1,0:T(8,128)(2,1)S(1)}, u32[]{:S(2)}, u32[]{:S(2)}) %collective-permute-start.14) | collective-permute-done | bytes 917536 | tf_op jit(solution)/shard_map/ppermute | solution.py:56
  113.5 1.3 fusion.63
  116.3 1.3 convolution_add_fusion.1
  118.2 3.6 %collective-permute-done.16 = bf16[2,2,32,3584]{3,2,1,0:T(8,128)(2,1)S(1)} collective-permute-done((bf16[2,2,32,3584]{3,2,1,0:T(8,128)(2,1)S(1)}, bf16[2,2,32,3584]{3,2,1,0:T(8,128)(2,1)S(1)}, u32[]{:S(2)}, u32[]{:S(2)}) %collective-permute-start.16) | collective-permute-done | bytes 917536 | tf_op jit(solution)/shard_map/ppermute | solution.py:56
  122.5 1.0 multiply_convert_fusion.3
  125.0 1.3 fusion.70
  126.4 1.3 convolution_add_fusion
  128.2 4.2 %collective-permute-start.12 = (bf16[32,3712]{1,0:T(8,128)(2,1)S(1)}, bf16[32,3712]{1,0:T(8,128)(2,1)S(1)}, u32[]{:S(2)}, u32[]{:S(2)}) collective-permute-start(bf16[32,3712]{1,0:T(8,128)(2,1)S(1)} %get-tuple-element.47), channel_id=1, source_target_pairs={{0,1},{1,0},{2,3},{3,2},{4,5},{5,4},{6,7},{7,6},{8,9},{9,8},{10,11... | collective-permute-start | bytes 712712 | tf_op jit(solution)/shard_map/ppermute | solution.py:56
  132.5 1.0 collective-permute-done.12
  134.4 1.4 collective-permute-done.19
  136.6 5.1 %collective-permute-start.20 = (bf16[32,3712]{1,0:T(8,128)(2,1)S(1)}, bf16[32,3712]{1,0:T(8,128)(2,1)S(1)}, u32[]{:S(2)}, u32[]{:S(2)}) collective-permute-start(bf16[32,3712]{1,0:T(8,128)(2,1)S(1)} %get-tuple-element.51), channel_id=1, source_target_pairs={{0,1},{1,0},{2,3},{3,2},{4,5},{5,4},{6,7},{7,6},{8,9},{9,8},{10,11... | collective-permute-start | bytes 712712 | tf_op jit(solution)/shard_map/ppermute | solution.py:56
  141.6 15.9 %collective-permute-done.17 = bf16[64,3712]{1,0:T(8,128)(2,1)S(1)} collective-permute-done((bf16[64,3712]{1,0:T(8,128)(2,1)S(1)}, bf16[64,3712]{1,0:T(8,128)(2,1)S(1)}, u32[]{:S(2)}, u32[]{:S(2)}) %collective-permute-start.17) | collective-permute-done | bytes 475168 | tf_op jit(solution)/shard_map/ppermute | solution.py:56
  157.5 2.2 %collective-permute-start.18 = (bf16[32,3712]{1,0:T(8,128)(2,1)S(1)}, bf16[32,3712]{1,0:T(8,128)(2,1)S(1)}, u32[]{:S(2)}, u32[]{:S(2)}) collective-permute-start(bf16[32,3712]{1,0:T(8,128)(2,1)S(1)} %get-tuple-element.49), channel_id=1, source_target_pairs={{0,1},{1,0},{2,3},{3,2},{4,5},{5,4},{6,7},{7,6},{8,9},{9,8},{10,11... | collective-permute-start | bytes 712712 | tf_op jit(solution)/shard_map/ppermute | solution.py:56
  162.6 1.1 fusion.4
  (117 shorter events, 23.2 us)
Async XLA Ops:
  0.6 1.6 copy-start
  0.6 2.3 %copy-start.4 = (bf16[128,3584]{1,0:T(8,128)(2,1)S(1)}, bf16[128,3584]{1,0:T(8,128)(2,1)}, u32[]{:S(2)}) copy-start(bf16[128,3584]{1,0:T(8,128)(2,1)} %param.8) | copy-start | bytes 2752516
  3.5 1.5 copy-start.2
  3.5 2.0 %copy-start.3 = (bf16[1,3584,256]{2,1,0:T(8,128)(2,1)S(1)}, bf16[1,3584,256]{2,1,0:T(8,128)(2,1)}, u32[]{:S(2)}) copy-start(bf16[1,3584,256]{2,1,0:T(8,128)(2,1)} %param.11) | copy-start | bytes 5505028
  3.9 4.6 %collective-permute-start = (bf16[4,2,32,3584]{3,2,0,1:T(8,128)(2,1)S(1)}, bf16[4,2,32,3584]{3,2,0,1:T(8,128)(2,1)S(1)}, u32[]{:S(2)}, u32[]{:S(2)}) collective-permute-start(bf16[4,2,32,3584]{3,2,0,1:T(8,128)(2,1)S(1)} %get-tuple-element.27), channel_id=1, source_target_pairs={{0,1},{1,0},{2,3},{3,2},{4,5},{5,4},{6,7},{7,6},{8,9},{9,8},{10,11... | collective-permute-start | bytes 5505032 | tf_op jit(solution)/shard_map/ppermute | solution.py:56
  5.6 1.6 copy-start.6
  5.9 67.5 %collective-permute-start.4 = (bf16[3584,512]{1,0:T(8,128)(2,1)S(1)}, bf16[3584,512]{1,0:T(8,128)(2,1)S(1)}, u32[]{:S(2)}, u32[]{:S(2)}) collective-permute-start(bf16[3584,512]{1,0:T(8,128)(2,1)S(1)} %pad_maximum_fusion), channel_id=1, source_target_pairs={{0,2},{1,5},{2,0},{3,7},{4,6},{5,1},{6,4},{7,3},{8,10},{9,13},{10,... | collective-permute-start | bytes 11010056 | tf_op jit(solution)/shard_map/ppermute | solution.py:56
  7.2 75.6 %collective-permute-start.3 = (bf16[256,3584]{1,0:T(8,128)(2,1)S(1)}, bf16[256,3584]{1,0:T(8,128)(2,1)S(1)}, u32[]{:S(2)}, u32[]{:S(2)}) collective-permute-start(bf16[256,3584]{1,0:T(8,128)(2,1)S(1)} %bitcast.129), channel_id=1, source_target_pairs={{0,2},{1,5},{2,0},{3,7},{4,6},{5,1},{6,4},{7,3},{8,10},{9,13},{10,... | collective-permute-start | bytes 5505032 | tf_op jit(solution)/shard_map/ppermute | solution.py:56
  8.8 39.2 %collective-permute-start.1 = (bf16[2,2,32,3584]{3,2,1,0:T(8,128)(2,1)S(1)}, bf16[2,2,32,3584]{3,2,1,0:T(8,128)(2,1)S(1)}, u32[]{:S(2)}, u32[]{:S(2)}) collective-permute-start(bf16[2,2,32,3584]{3,2,1,0:T(8,128)(2,1)S(1)} %get-tuple-element.23), channel_id=1, source_target_pairs={{0,16},{1,17},{2,18},{3,19},{4,20},{5,21},{6,22},{7,23},{8,24},{9,... | collective-permute-start | bytes 2752520 | tf_op jit(solution)/shard_map/ppermute | solution.py:56
  9.0 41.2 %collective-permute-start.6 = (bf16[2,2,32,3584]{3,2,1,0:T(8,128)(2,1)S(1)}, bf16[2,2,32,3584]{3,2,1,0:T(8,128)(2,1)S(1)}, u32[]{:S(2)}, u32[]{:S(2)}) collective-permute-start(bf16[2,2,32,3584]{3,2,1,0:T(8,128)(2,1)S(1)} %get-tuple-element.22), channel_id=1, source_target_pairs={{0,8},{1,9},{2,10},{3,11},{4,12},{5,13},{6,14},{7,15},{8,0},{9,1},... | collective-permute-start | bytes 2752520 | tf_op jit(solution)/shard_map/ppermute | solution.py:56
  48.1 22.4 %collective-permute-start.2 = (bf16[2,2,32,3584]{3,2,1,0:T(8,128)(2,1)S(1)}, bf16[2,2,32,3584]{3,2,1,0:T(8,128)(2,1)S(1)}, u32[]{:S(2)}, u32[]{:S(2)}) collective-permute-start(bf16[2,2,32,3584]{3,2,1,0:T(8,128)(2,1)S(1)} %collective-permute-done.1), channel_id=1, source_target_pairs={{0,4},{1,3},{2,6},{3,1},{4,0},{5,7},{6,2},{7,5},{8,12},{9,11},{10,... | collective-permute-start | bytes 2752520 | tf_op jit(solution)/shard_map/ppermute | solution.py:56
  50.1 38.3 %collective-permute-start.7 = (bf16[2,2,32,3584]{3,2,1,0:T(8,128)(2,1)S(1)}, bf16[2,2,32,3584]{3,2,1,0:T(8,128)(2,1)S(1)}, u32[]{:S(2)}, u32[]{:S(2)}) collective-permute-start(bf16[2,2,32,3584]{3,2,1,0:T(8,128)(2,1)S(1)} %collective-permute-done.6), channel_id=1, source_target_pairs={{0,4},{1,3},{2,6},{3,1},{4,0},{5,7},{6,2},{7,5},{8,12},{9,11},{10,... | collective-permute-start | bytes 2752520 | tf_op jit(solution)/shard_map/ppermute | solution.py:56
  50.1 44.5 %collective-permute-start.13 = (bf16[2,2,32,3584]{3,2,1,0:T(8,128)(2,1)S(1)}, bf16[2,2,32,3584]{3,2,1,0:T(8,128)(2,1)S(1)}, u32[]{:S(2)}, u32[]{:S(2)}) collective-permute-start(bf16[2,2,32,3584]{3,2,1,0:T(8,128)(2,1)S(1)} %get-tuple-element.15), channel_id=1, source_target_pairs={{0,24},{1,25},{2,26},{3,27},{4,28},{5,29},{6,30},{7,31},{8,16},{9,... | collective-permute-start | bytes 2752520 | tf_op jit(solution)/shard_map/ppermute | solution.py:56
  85.2 10.9 %collective-permute-start.5 = (bf16[64,3712]{1,0:T(8,128)(2,1)S(1)}, bf16[64,3712]{1,0:T(8,128)(2,1)S(1)}, u32[]{:S(2)}, u32[]{:S(2)}) collective-permute-start(bf16[64,3712]{1,0:T(8,128)(2,1)S(1)} %pad_maximum_fusion.27), channel_id=1, source_target_pairs={{0,4},{1,3},{2,6},{3,1},{4,0},{5,7},{6,2},{7,5},{8,12},{9,11},{10,... | collective-permute-start | bytes 1425416 | tf_op jit(solution)/shard_map/ppermute | solution.py:56
  94.3 7.9 %collective-permute-start.10 = (bf16[64,3712]{1,0:T(8,128)(2,1)S(1)}, bf16[64,3712]{1,0:T(8,128)(2,1)S(1)}, u32[]{:S(2)}, u32[]{:S(2)}) collective-permute-start(bf16[64,3712]{1,0:T(8,128)(2,1)S(1)} %pad_maximum_fusion.28), channel_id=1, source_target_pairs={{0,4},{1,3},{2,6},{3,1},{4,0},{5,7},{6,2},{7,5},{8,12},{9,11},{10,... | collective-permute-start | bytes 1425416 | tf_op jit(solution)/shard_map/ppermute | solution.py:56
  94.6 17.4 %collective-permute-start.14 = (bf16[2,2,32,3584]{3,2,1,0:T(8,128)(2,1)S(1)}, bf16[2,2,32,3584]{3,2,1,0:T(8,128)(2,1)S(1)}, u32[]{:S(2)}, u32[]{:S(2)}) collective-permute-start(bf16[2,2,32,3584]{3,2,1,0:T(8,128)(2,1)S(1)} %collective-permute-done.13), channel_id=1, source_target_pairs={{0,4},{1,3},{2,6},{3,1},{4,0},{5,7},{6,2},{7,5},{8,12},{9,11},{10,... | collective-permute-start | bytes 2752520 | tf_op jit(solution)/shard_map/ppermute | solution.py:56
  95.8 26.0 %collective-permute-start.16 = (bf16[2,2,32,3584]{3,2,1,0:T(8,128)(2,1)S(1)}, bf16[2,2,32,3584]{3,2,1,0:T(8,128)(2,1)S(1)}, u32[]{:S(2)}, u32[]{:S(2)}) collective-permute-start(bf16[2,2,32,3584]{3,2,1,0:T(8,128)(2,1)S(1)} %get-tuple-element.18), channel_id=1, source_target_pairs={{0,4},{1,3},{2,6},{3,1},{4,0},{5,7},{6,2},{7,5},{8,12},{9,11},{10,... | collective-permute-start | bytes 2752520 | tf_op jit(solution)/shard_map/ppermute | solution.py:56
  102.7 29.7 %collective-permute-start.8 = (bf16[64,3712]{1,0:T(8,128)(2,1)S(1)}, bf16[64,3712]{1,0:T(8,128)(2,1)S(1)}, u32[]{:S(2)}, u32[]{:S(2)}) collective-permute-start(bf16[64,3712]{1,0:T(8,128)(2,1)S(1)} %pad_maximum_fusion.29), channel_id=1, source_target_pairs={{0,16},{1,17},{2,18},{3,19},{4,20},{5,21},{6,22},{7,23},{8,24},{9,... | collective-permute-start | bytes 1425416 | tf_op jit(solution)/shard_map/ppermute | solution.py:56
  102.8 25.3 %collective-permute-start.11 = (bf16[64,3712]{1,0:T(8,128)(2,1)S(1)}, bf16[64,3712]{1,0:T(8,128)(2,1)S(1)}, u32[]{:S(2)}, u32[]{:S(2)}) collective-permute-start(bf16[64,3712]{1,0:T(8,128)(2,1)S(1)} %pad_maximum_fusion.30), channel_id=1, source_target_pairs={{0,8},{1,9},{2,10},{3,11},{4,12},{5,13},{6,14},{7,15},{8,0},{9,1},... | collective-permute-start | bytes 1425416 | tf_op jit(solution)/shard_map/ppermute | solution.py:56
  117.9 16.1 %collective-permute-start.15 = (bf16[64,3712]{1,0:T(8,128)(2,1)S(1)}, bf16[64,3712]{1,0:T(8,128)(2,1)S(1)}, u32[]{:S(2)}, u32[]{:S(2)}) collective-permute-start(bf16[64,3712]{1,0:T(8,128)(2,1)S(1)} %pad_maximum_fusion.31), channel_id=1, source_target_pairs={{0,4},{1,3},{2,6},{3,1},{4,0},{5,7},{6,2},{7,5},{8,12},{9,11},{10,... | collective-permute-start | bytes 1425416 | tf_op jit(solution)/shard_map/ppermute | solution.py:56
  127.9 7.9 %collective-permute-start.19 = (bf16[64,3712]{1,0:T(8,128)(2,1)S(1)}, bf16[64,3712]{1,0:T(8,128)(2,1)S(1)}, u32[]{:S(2)}, u32[]{:S(2)}) collective-permute-start(bf16[64,3712]{1,0:T(8,128)(2,1)S(1)} %pad_maximum_fusion.32), channel_id=1, source_target_pairs={{0,4},{1,3},{2,6},{3,1},{4,0},{5,7},{6,2},{7,5},{8,12},{9,11},{10,... | collective-permute-start | bytes 1425416 | tf_op jit(solution)/shard_map/ppermute | solution.py:56
  128.2 5.3 %collective-permute-start.12 = (bf16[32,3712]{1,0:T(8,128)(2,1)S(1)}, bf16[32,3712]{1,0:T(8,128)(2,1)S(1)}, u32[]{:S(2)}, u32[]{:S(2)}) collective-permute-start(bf16[32,3712]{1,0:T(8,128)(2,1)S(1)} %get-tuple-element.47), channel_id=1, source_target_pairs={{0,1},{1,0},{2,3},{3,2},{4,5},{5,4},{6,7},{7,6},{8,9},{9,8},{10,11... | collective-permute-start | bytes 712712 | tf_op jit(solution)/shard_map/ppermute | solution.py:56
  132.4 28.9 %collective-permute-start.9 = (bf16[32,3712]{1,0:T(8,128)(2,1)S(1)}, bf16[32,3712]{1,0:T(8,128)(2,1)S(1)}, u32[]{:S(2)}, u32[]{:S(2)}) collective-permute-start(bf16[32,3712]{1,0:T(8,128)(2,1)S(1)} %get-tuple-element.45), channel_id=1, source_target_pairs={{0,1},{1,0},{2,3},{3,2},{4,5},{5,4},{6,7},{7,6},{8,9},{9,8},{10,11... | collective-permute-start | bytes 712712 | tf_op jit(solution)/shard_map/ppermute | solution.py:56
  136.2 21.4 %collective-permute-start.17 = (bf16[64,3712]{1,0:T(8,128)(2,1)S(1)}, bf16[64,3712]{1,0:T(8,128)(2,1)S(1)}, u32[]{:S(2)}, u32[]{:S(2)}) collective-permute-start(bf16[64,3712]{1,0:T(8,128)(2,1)S(1)} %pad_maximum_fusion.33), channel_id=1, source_target_pairs={{0,24},{1,25},{2,26},{3,27},{4,28},{5,29},{6,30},{7,31},{8,16},{9,... | collective-permute-start | bytes 1425416 | tf_op jit(solution)/shard_map/ppermute | solution.py:56
  136.6 23.2 %collective-permute-start.20 = (bf16[32,3712]{1,0:T(8,128)(2,1)S(1)}, bf16[32,3712]{1,0:T(8,128)(2,1)S(1)}, u32[]{:S(2)}, u32[]{:S(2)}) collective-permute-start(bf16[32,3712]{1,0:T(8,128)(2,1)S(1)} %get-tuple-element.51), channel_id=1, source_target_pairs={{0,1},{1,0},{2,3},{3,2},{4,5},{5,4},{6,7},{7,6},{8,9},{9,8},{10,11... | collective-permute-start | bytes 712712 | tf_op jit(solution)/shard_map/ppermute | solution.py:56
  157.5 3.4 %collective-permute-start.18 = (bf16[32,3712]{1,0:T(8,128)(2,1)S(1)}, bf16[32,3712]{1,0:T(8,128)(2,1)S(1)}, u32[]{:S(2)}, u32[]{:S(2)}) collective-permute-start(bf16[32,3712]{1,0:T(8,128)(2,1)S(1)} %get-tuple-element.49), channel_id=1, source_target_pairs={{0,1},{1,0},{2,3},{3,2},{4,5},{5,4},{6,7},{7,6},{8,9},{9,8},{10,11... | collective-permute-start | bytes 712712 | tf_op jit(solution)/shard_map/ppermute | solution.py:56
  161.4 1.2 copy-start.5
  161.4 2.3 %copy-start.1 = (bf16[128,3584]{1,0:T(8,128)(2,1)S(1)}, bf16[128,3584]{1,0:T(8,128)(2,1)}, u32[]{:S(2)}) copy-start(bf16[128,3584]{1,0:T(8,128)(2,1)} %param.7) | copy-start | bytes 2752516

commit v3 on v2

--- a/solution.py
+++ b/solution.py
@@ -138,18 +138,23 @@
     totals = [None] * blocks
     swap_in(0)
     swap_in(1)
-    for first in range(0, blocks, 2):
-        last = min(first + 1, blocks - 1)
-        for i in range(first, last + 1):
-            wait = [parts[i - 1][2]] if i > first else []
-            if i == first and i > 0:
-                wait.append(totals[i - 1])
-            parts[i] = compute(i, *wait)
-            if i == first:
-                for j in range(last + 1, min(last + 3, blocks)):
-                    swap_in(j, parts[i][2], arrived[min(last + 1, blocks - 1)])
-        for i in range(first, last + 1):
-            totals[i] = finish(i, parts[i], parts[last][2])
+    for i in range(blocks):
+        last = i == blocks - 1
+        if i > 1:
+            swap_in(i, parts[i - 1 if last else i - 2][2])
+        if i == 0:
+            wait = []
+        elif i == 1 or last:
+            wait = [totals[i - 1]]
+        else:
+            wait = [parts[i - 1][2]]
+        parts[i] = compute(i, *wait)
+        if i == 0:
+            totals[i] = finish(i, parts[i], *arrived[2:3])
+        if i > 1 and not last:
+            totals[i - 1] = finish(i - 1, parts[i - 1], parts[i][2])
+        if i > 0 and i >= blocks - 2:
+            totals[i] = finish(i, parts[i])
 
     rows = 0.0
     select = select.T.reshape(count, blocks, half).astype(jnp.bfloat16)

time: 164 us -> 151 us (0.921); the launches traced: 164 us -> 149 us
  waiting for transfers between devices: 105 us -> 91.5 us
    ppermute x21, waiting for transfers between devices: 105 us -> 91.5 us  [permute(): return lax.ppermute(value, AXES, pairs)]
  transfers between devices with their start and end apart: 21 -> 21, of which waited for: 12 -> 11; matrix products, arithmetic and copies ran while one was open for 17% -> 19% of each run, Pallas kernels for 0% -> 0%
where the time goes in v3:
time: 151 us; the launch traced here: 149 us
  waiting for transfers between devices  91.5 us (61%)
  matrix products  25.3 us (17%)
  starting transfers between devices  22.2 us (15%)
  other arithmetic  7.05 us (5%)
  local copies, waits for them, and re-layouts  1.78 us (1%)
    ppermute x21, waiting for transfers between devices, permute(): return lax.ppermute(value, AXES, pairs)  91.5 us
    ppermute x21, starting transfers between devices, permute(): return lax.ppermute(value, AXES, pairs)  22.2 us
    dot_general x16, matrix products, times_transposed(): lax.dot_general(left, right, (((1,), (1,)), ((), ())), preferred_element_...  16.8 us
    dot_general x14, matrix products, times(): return jnp.dot(left, right, preferred_element_type=jnp.float32)  8.45 us
  transfers between devices with their start and end apart: 21, of which 11 were waited for; matrix products, arithmetic and copies ran while one was open for 19% of the time, Pallas kernels for 0%

profile of v3, /device:TPU:19, one launch (start us, length us, event | category | flops | bytes accessed | tf_op | source)
XLA Modules:
  0.0 149.0 jit_solution(13396851059626088543)
XLA Ops:
  0.7 0.9 convert_reduce_fusion
  5.9 1.3 collective-permute-start.4
  7.2 1.1 collective-permute-start.3
  9.0 1.3 collective-permute-start.9
  10.3 37.7 %collective-permute-done.1 = bf16[2,2,32,3584]{3,2,1,0:T(8,128)(2,1)S(1)} collective-permute-done((bf16[2,2,32,3584]{3,2,1,0:T(8,128)(2,1)S(1)}, bf16[2,2,32,3584]{3,2,1,0:T(8,128)(2,1)S(1)}, u32[]{:S(2)}, u32[]{:S(2)}) %collective-permute-start.1) | collective-permute-done | bytes 917536 | tf_op jit(solution)/shard_map/ppermute | solution.py:56
  48.1 2.9 %collective-permute-start.6 = (bf16[2,2,32,3584]{3,2,1,0:T(8,128)(2,1)S(1)}, bf16[2,2,32,3584]{3,2,1,0:T(8,128)(2,1)S(1)}, u32[]{:S(2)}, u32[]{:S(2)}) collective-permute-start(bf16[2,2,32,3584]{3,2,1,0:T(8,128)(2,1)S(1)} %get-tuple-element.10), channel_id=1, source_target_pairs={{0,24},{1,25},{2,26},{3,27},{4,28},{5,29},{6,30},{7,31},{8,16},{9,... | collective-permute-start | bytes 2752520 | tf_op jit(solution)/shard_map/ppermute | solution.py:56
  51.3 1.2 collective-permute-start.10
  52.6 20.8 %collective-permute-done.2 = bf16[2,2,32,3584]{3,2,1,0:T(8,128)(2,1)S(1)} collective-permute-done((bf16[2,2,32,3584]{3,2,1,0:T(8,128)(2,1)S(1)}, bf16[2,2,32,3584]{3,2,1,0:T(8,128)(2,1)S(1)}, u32[]{:S(2)}, u32[]{:S(2)}) %collective-permute-start.2) | collective-permute-done | bytes 917536 | tf_op jit(solution)/shard_map/ppermute | solution.py:56
  75.0 1.3 fusion.49
  76.9 3.3 %collective-permute-done.3 = bf16[256,3584]{1,0:T(8,128)(2,1)S(1)} collective-permute-done((bf16[256,3584]{1,0:T(8,128)(2,1)S(1)}, bf16[256,3584]{1,0:T(8,128)(2,1)S(1)}, u32[]{:S(2)}, u32[]{:S(2)}) %collective-permute-start.3) | collective-permute-done | bytes 1835040 | tf_op jit(solution)/shard_map/ppermute | solution.py:56
  81.0 1.3 convolution_add_fusion.3
  83.0 8.0 %collective-permute-done.6 = bf16[2,2,32,3584]{3,2,1,0:T(8,128)(2,1)S(1)} collective-permute-done((bf16[2,2,32,3584]{3,2,1,0:T(8,128)(2,1)S(1)}, bf16[2,2,32,3584]{3,2,1,0:T(8,128)(2,1)S(1)}, u32[]{:S(2)}, u32[]{:S(2)}) %collective-permute-start.6) | collective-permute-done | bytes 917536 | tf_op jit(solution)/shard_map/ppermute | solution.py:56
  91.3 2.3 %collective-permute-done.5 = bf16[64,3712]{1,0:T(8,128)(2,1)S(1)} collective-permute-done((bf16[64,3712]{1,0:T(8,128)(2,1)S(1)}, bf16[64,3712]{1,0:T(8,128)(2,1)S(1)}, u32[]{:S(2)}, u32[]{:S(2)}) %collective-permute-start.5) | collective-permute-done | bytes 475168 | tf_op jit(solution)/shard_map/ppermute | solution.py:56
  95.7 1.3 fusion.56
  98.4 1.3 convolution_add_fusion.2
  100.3 3.2 %collective-permute-done.12 = bf16[2,2,32,3584]{3,2,1,0:T(8,128)(2,1)S(1)} collective-permute-done((bf16[2,2,32,3584]{3,2,1,0:T(8,128)(2,1)S(1)}, bf16[2,2,32,3584]{3,2,1,0:T(8,128)(2,1)S(1)}, u32[]{:S(2)}, u32[]{:S(2)}) %collective-permute-start.12) | collective-permute-done | bytes 917536 | tf_op jit(solution)/shard_map/ppermute | solution.py:56
  106.6 1.3 fusion.63
  107.9 1.3 convolution_add_fusion.1
  109.7 1.2 collective-permute-start.18
  111.1 2.8 %collective-permute-done.7 = bf16[64,3712]{1,0:T(8,128)(2,1)S(1)} collective-permute-done((bf16[64,3712]{1,0:T(8,128)(2,1)S(1)}, bf16[64,3712]{1,0:T(8,128)(2,1)S(1)}, u32[]{:S(2)}, u32[]{:S(2)}) %collective-permute-start.7) | collective-permute-done | bytes 475168 | tf_op jit(solution)/shard_map/ppermute | solution.py:56
  113.9 1.6 %collective-permute-start.8 = (bf16[32,3712]{1,0:T(8,128)(2,1)S(1)}, bf16[32,3712]{1,0:T(8,128)(2,1)S(1)}, u32[]{:S(2)}, u32[]{:S(2)}) collective-permute-start(bf16[32,3712]{1,0:T(8,128)(2,1)S(1)} %get-tuple-element.41), channel_id=1, source_target_pairs={{0,1},{1,0},{2,3},{3,2},{4,5},{5,4},{6,7},{7,6},{8,9},{9,8},{10,11... | collective-permute-start | bytes 712712 | tf_op jit(solution)/shard_map/ppermute | solution.py:56
  115.7 1.5 %collective-permute-done.15 = bf16[64,3712]{1,0:T(8,128)(2,1)S(1)} collective-permute-done((bf16[64,3712]{1,0:T(8,128)(2,1)S(1)}, bf16[64,3712]{1,0:T(8,128)(2,1)S(1)}, u32[]{:S(2)}, u32[]{:S(2)}) %collective-permute-start.15) | collective-permute-done | bytes 475168 | tf_op jit(solution)/shard_map/ppermute | solution.py:56
  117.7 1.2 collective-permute-start.16
  119.0 1.7 %collective-permute-start.13 = (bf16[64,3712]{1,0:T(8,128)(2,1)S(1)}, bf16[64,3712]{1,0:T(8,128)(2,1)S(1)}, u32[]{:S(2)}, u32[]{:S(2)}) collective-permute-start(bf16[64,3712]{1,0:T(8,128)(2,1)S(1)} %pad_maximum_fusion.31), channel_id=1, source_target_pairs={{0,8},{1,9},{2,10},{3,11},{4,12},{5,13},{6,14},{7,15},{8,0},{9,1},... | collective-permute-start | bytes 1425416 | tf_op jit(solution)/shard_map/ppermute | solution.py:56
  120.7 6.4 %collective-permute-done.18 = bf16[2,2,32,3584]{3,2,1,0:T(8,128)(2,1)S(1)} collective-permute-done((bf16[2,2,32,3584]{3,2,1,0:T(8,128)(2,1)S(1)}, bf16[2,2,32,3584]{3,2,1,0:T(8,128)(2,1)S(1)}, u32[]{:S(2)}, u32[]{:S(2)}) %collective-permute-start.18) | collective-permute-done | bytes 917536 | tf_op jit(solution)/shard_map/ppermute | solution.py:56
  130.3 1.3 fusion.70
  131.6 1.3 convolution_add_fusion
  133.4 4.9 %collective-permute-done.16 = bf16[64,3712]{1,0:T(8,128)(2,1)S(1)} collective-permute-done((bf16[64,3712]{1,0:T(8,128)(2,1)S(1)}, bf16[64,3712]{1,0:T(8,128)(2,1)S(1)}, u32[]{:S(2)}, u32[]{:S(2)}) %collective-permute-start.16) | collective-permute-done | bytes 475168 | tf_op jit(solution)/shard_map/ppermute | solution.py:56
  138.3 3.0 %collective-permute-start.17 = (bf16[32,3712]{1,0:T(8,128)(2,1)S(1)}, bf16[32,3712]{1,0:T(8,128)(2,1)S(1)}, u32[]{:S(2)}, u32[]{:S(2)}) collective-permute-start(bf16[32,3712]{1,0:T(8,128)(2,1)S(1)} %get-tuple-element.45), channel_id=1, source_target_pairs={{0,1},{1,0},{2,3},{3,2},{4,5},{5,4},{6,7},{7,6},{8,9},{9,8},{10,11... | collective-permute-start | bytes 712712 | tf_op jit(solution)/shard_map/ppermute | solution.py:56
  141.4 1.4 collective-permute-start.14
  143.8 1.4 collective-permute-start.20
  147.9 1.1 fusion.4
  (118 shorter events, 25.0 us)
Async XLA Ops:
  0.6 1.6 %copy-start = (bf16[128,3584]{1,0:T(8,128)(2,1)S(1)}, bf16[128,3584]{1,0:T(8,128)(2,1)}, u32[]{:S(2)}) copy-start(bf16[128,3584]{1,0:T(8,128)(2,1)} %param.7) | copy-start | bytes 2752516
  0.6 2.2 %copy-start.4 = (bf16[128,3584]{1,0:T(8,128)(2,1)S(1)}, bf16[128,3584]{1,0:T(8,128)(2,1)}, u32[]{:S(2)}) copy-start(bf16[128,3584]{1,0:T(8,128)(2,1)} %param.8) | copy-start | bytes 2752516
  3.5 1.5 %copy-start.2 = (bf16[1,3584,256]{2,1,0:T(8,128)(2,1)S(1)}, bf16[1,3584,256]{2,1,0:T(8,128)(2,1)}, u32[]{:S(2)}) copy-start(bf16[1,3584,256]{2,1,0:T(8,128)(2,1)} %param.12) | copy-start | bytes 5505028
  3.5 2.0 %copy-start.3 = (bf16[1,3584,256]{2,1,0:T(8,128)(2,1)S(1)}, bf16[1,3584,256]{2,1,0:T(8,128)(2,1)}, u32[]{:S(2)}) copy-start(bf16[1,3584,256]{2,1,0:T(8,128)(2,1)} %param.11) | copy-start | bytes 5505028
  3.9 4.6 %collective-permute-start = (bf16[4,2,32,3584]{3,2,0,1:T(8,128)(2,1)S(1)}, bf16[4,2,32,3584]{3,2,0,1:T(8,128)(2,1)S(1)}, u32[]{:S(2)}, u32[]{:S(2)}) collective-permute-start(bf16[4,2,32,3584]{3,2,0,1:T(8,128)(2,1)S(1)} %get-tuple-element.23), channel_id=1, source_target_pairs={{0,1},{1,0},{2,3},{3,2},{4,5},{5,4},{6,7},{7,6},{8,9},{9,8},{10,11... | collective-permute-start | bytes 5505032 | tf_op jit(solution)/shard_map/ppermute | solution.py:56
  5.6 1.6 %copy-start.6 = (bf16[1,256,3584]{2,1,0:T(8,128)(2,1)S(1)}, bf16[1,256,3584]{2,1,0:T(8,128)(2,1)}, u32[]{:S(2)}) copy-start(bf16[1,256,3584]{2,1,0:T(8,128)(2,1)} %param.13) | copy-start | bytes 5505028
  5.9 70.4 %collective-permute-start.4 = (bf16[3584,512]{1,0:T(8,128)(2,1)S(1)}, bf16[3584,512]{1,0:T(8,128)(2,1)S(1)}, u32[]{:S(2)}, u32[]{:S(2)}) collective-permute-start(bf16[3584,512]{1,0:T(8,128)(2,1)S(1)} %pad_maximum_fusion), channel_id=1, source_target_pairs={{0,2},{1,5},{2,0},{3,7},{4,6},{5,1},{6,4},{7,3},{8,10},{9,13},{10,... | collective-permute-start | bytes 11010056 | tf_op jit(solution)/shard_map/ppermute | solution.py:56
  7.2 73.1 %collective-permute-start.3 = (bf16[256,3584]{1,0:T(8,128)(2,1)S(1)}, bf16[256,3584]{1,0:T(8,128)(2,1)S(1)}, u32[]{:S(2)}, u32[]{:S(2)}) collective-permute-start(bf16[256,3584]{1,0:T(8,128)(2,1)S(1)} %bitcast.129), channel_id=1, source_target_pairs={{0,2},{1,5},{2,0},{3,7},{4,6},{5,1},{6,4},{7,3},{8,10},{9,13},{10,... | collective-permute-start | bytes 5505032 | tf_op jit(solution)/shard_map/ppermute | solution.py:56
  8.8 39.2 %collective-permute-start.1 = (bf16[2,2,32,3584]{3,2,1,0:T(8,128)(2,1)S(1)}, bf16[2,2,32,3584]{3,2,1,0:T(8,128)(2,1)S(1)}, u32[]{:S(2)}, u32[]{:S(2)}) collective-permute-start(bf16[2,2,32,3584]{3,2,1,0:T(8,128)(2,1)S(1)} %get-tuple-element.19), channel_id=1, source_target_pairs={{0,16},{1,17},{2,18},{3,19},{4,20},{5,21},{6,22},{7,23},{8,24},{9,... | collective-permute-start | bytes 2752520 | tf_op jit(solution)/shard_map/ppermute | solution.py:56
  9.0 42.3 %collective-permute-start.9 = (bf16[2,2,32,3584]{3,2,1,0:T(8,128)(2,1)S(1)}, bf16[2,2,32,3584]{3,2,1,0:T(8,128)(2,1)S(1)}, u32[]{:S(2)}, u32[]{:S(2)}) collective-permute-start(bf16[2,2,32,3584]{3,2,1,0:T(8,128)(2,1)S(1)} %get-tuple-element.18), channel_id=1, source_target_pairs={{0,8},{1,9},{2,10},{3,11},{4,12},{5,13},{6,14},{7,15},{8,0},{9,1},... | collective-permute-start | bytes 2752520 | tf_op jit(solution)/shard_map/ppermute | solution.py:56
  48.1 42.9 %collective-permute-start.6 = (bf16[2,2,32,3584]{3,2,1,0:T(8,128)(2,1)S(1)}, bf16[2,2,32,3584]{3,2,1,0:T(8,128)(2,1)S(1)}, u32[]{:S(2)}, u32[]{:S(2)}) collective-permute-start(bf16[2,2,32,3584]{3,2,1,0:T(8,128)(2,1)S(1)} %get-tuple-element.10), channel_id=1, source_target_pairs={{0,24},{1,25},{2,26},{3,27},{4,28},{5,29},{6,30},{7,31},{8,16},{9,... | collective-permute-start | bytes 2752520 | tf_op jit(solution)/shard_map/ppermute | solution.py:56
  51.0 22.4 %collective-permute-start.2 = (bf16[2,2,32,3584]{3,2,1,0:T(8,128)(2,1)S(1)}, bf16[2,2,32,3584]{3,2,1,0:T(8,128)(2,1)S(1)}, u32[]{:S(2)}, u32[]{:S(2)}) collective-permute-start(bf16[2,2,32,3584]{3,2,1,0:T(8,128)(2,1)S(1)} %collective-permute-done.1), channel_id=1, source_target_pairs={{0,4},{1,3},{2,6},{3,1},{4,0},{5,7},{6,2},{7,5},{8,12},{9,11},{10,... | collective-permute-start | bytes 2752520 | tf_op jit(solution)/shard_map/ppermute | solution.py:56
  51.3 42.9 %collective-permute-start.10 = (bf16[2,2,32,3584]{3,2,1,0:T(8,128)(2,1)S(1)}, bf16[2,2,32,3584]{3,2,1,0:T(8,128)(2,1)S(1)}, u32[]{:S(2)}, u32[]{:S(2)}) collective-permute-start(bf16[2,2,32,3584]{3,2,1,0:T(8,128)(2,1)S(1)} %collective-permute-done.9), channel_id=1, source_target_pairs={{0,4},{1,3},{2,6},{3,1},{4,0},{5,7},{6,2},{7,5},{8,12},{9,11},{10,... | collective-permute-start | bytes 2752520 | tf_op jit(solution)/shard_map/ppermute | solution.py:56
  82.6 10.9 %collective-permute-start.5 = (bf16[64,3712]{1,0:T(8,128)(2,1)S(1)}, bf16[64,3712]{1,0:T(8,128)(2,1)S(1)}, u32[]{:S(2)}, u32[]{:S(2)}) collective-permute-start(bf16[64,3712]{1,0:T(8,128)(2,1)S(1)} %pad_maximum_fusion.27), channel_id=1, source_target_pairs={{0,4},{1,3},{2,6},{3,1},{4,0},{5,7},{6,2},{7,5},{8,12},{9,11},{10,... | collective-permute-start | bytes 1425416 | tf_op jit(solution)/shard_map/ppermute | solution.py:56
  91.0 12.5 %collective-permute-start.12 = (bf16[2,2,32,3584]{3,2,1,0:T(8,128)(2,1)S(1)}, bf16[2,2,32,3584]{3,2,1,0:T(8,128)(2,1)S(1)}, u32[]{:S(2)}, u32[]{:S(2)}) collective-permute-start(bf16[2,2,32,3584]{3,2,1,0:T(8,128)(2,1)S(1)} %collective-permute-done.6), channel_id=1, source_target_pairs={{0,4},{1,3},{2,6},{3,1},{4,0},{5,7},{6,2},{7,5},{8,12},{9,11},{10,... | collective-permute-start | bytes 2752520 | tf_op jit(solution)/shard_map/ppermute | solution.py:56
  94.0 19.8 %collective-permute-start.7 = (bf16[64,3712]{1,0:T(8,128)(2,1)S(1)}, bf16[64,3712]{1,0:T(8,128)(2,1)S(1)}, u32[]{:S(2)}, u32[]{:S(2)}) collective-permute-start(bf16[64,3712]{1,0:T(8,128)(2,1)S(1)} %pad_maximum_fusion.28), channel_id=1, source_target_pairs={{0,16},{1,17},{2,18},{3,19},{4,20},{5,21},{6,22},{7,23},{8,24},{9,... | collective-permute-start | bytes 1425416 | tf_op jit(solution)/shard_map/ppermute | solution.py:56
  100.0 10.9 %collective-permute-start.11 = (bf16[64,3712]{1,0:T(8,128)(2,1)S(1)}, bf16[64,3712]{1,0:T(8,128)(2,1)S(1)}, u32[]{:S(2)}, u32[]{:S(2)}) collective-permute-start(bf16[64,3712]{1,0:T(8,128)(2,1)S(1)} %pad_maximum_fusion.29), channel_id=1, source_target_pairs={{0,4},{1,3},{2,6},{3,1},{4,0},{5,7},{6,2},{7,5},{8,12},{9,11},{10,... | collective-permute-start | bytes 1425416 | tf_op jit(solution)/shard_map/ppermute | solution.py:56
  109.4 7.9 %collective-permute-start.15 = (bf16[64,3712]{1,0:T(8,128)(2,1)S(1)}, bf16[64,3712]{1,0:T(8,128)(2,1)S(1)}, u32[]{:S(2)}, u32[]{:S(2)}) collective-permute-start(bf16[64,3712]{1,0:T(8,128)(2,1)S(1)} %pad_maximum_fusion.30), channel_id=1, source_target_pairs={{0,4},{1,3},{2,6},{3,1},{4,0},{5,7},{6,2},{7,5},{8,12},{9,11},{10,... | collective-permute-start | bytes 1425416 | tf_op jit(solution)/shard_map/ppermute | solution.py:56
  109.7 17.4 %collective-permute-start.18 = (bf16[2,2,32,3584]{3,2,1,0:T(8,128)(2,1)S(1)}, bf16[2,2,32,3584]{3,2,1,0:T(8,128)(2,1)S(1)}, u32[]{:S(2)}, u32[]{:S(2)}) collective-permute-start(bf16[2,2,32,3584]{3,2,1,0:T(8,128)(2,1)S(1)} %get-tuple-element.16), channel_id=1, source_target_pairs={{0,4},{1,3},{2,6},{3,1},{4,0},{5,7},{6,2},{7,5},{8,12},{9,11},{10,... | collective-permute-start | bytes 2752520 | tf_op jit(solution)/shard_map/ppermute | solution.py:56
  113.9 32.8 %collective-permute-start.8 = (bf16[32,3712]{1,0:T(8,128)(2,1)S(1)}, bf16[32,3712]{1,0:T(8,128)(2,1)S(1)}, u32[]{:S(2)}, u32[]{:S(2)}) collective-permute-start(bf16[32,3712]{1,0:T(8,128)(2,1)S(1)} %get-tuple-element.41), channel_id=1, source_target_pairs={{0,1},{1,0},{2,3},{3,2},{4,5},{5,4},{6,7},{7,6},{8,9},{9,8},{10,11... | collective-permute-start | bytes 712712 | tf_op jit(solution)/shard_map/ppermute | solution.py:56
  117.7 20.6 %collective-permute-start.16 = (bf16[64,3712]{1,0:T(8,128)(2,1)S(1)}, bf16[64,3712]{1,0:T(8,128)(2,1)S(1)}, u32[]{:S(2)}, u32[]{:S(2)}) collective-permute-start(bf16[64,3712]{1,0:T(8,128)(2,1)S(1)} %pad_maximum_fusion.32), channel_id=1, source_target_pairs={{0,24},{1,25},{2,26},{3,27},{4,28},{5,29},{6,30},{7,31},{8,16},{9,... | collective-permute-start | bytes 1425416 | tf_op jit(solution)/shard_map/ppermute | solution.py:56
  119.0 22.4 %collective-permute-start.13 = (bf16[64,3712]{1,0:T(8,128)(2,1)S(1)}, bf16[64,3712]{1,0:T(8,128)(2,1)S(1)}, u32[]{:S(2)}, u32[]{:S(2)}) collective-permute-start(bf16[64,3712]{1,0:T(8,128)(2,1)S(1)} %pad_maximum_fusion.31), channel_id=1, source_target_pairs={{0,8},{1,9},{2,10},{3,11},{4,12},{5,13},{6,14},{7,15},{8,0},{9,1},... | collective-permute-start | bytes 1425416 | tf_op jit(solution)/shard_map/ppermute | solution.py:56
  133.1 10.1 %collective-permute-start.19 = (bf16[64,3712]{1,0:T(8,128)(2,1)S(1)}, bf16[64,3712]{1,0:T(8,128)(2,1)S(1)}, u32[]{:S(2)}, u32[]{:S(2)}) collective-permute-start(bf16[64,3712]{1,0:T(8,128)(2,1)S(1)} %pad_maximum_fusion.33), channel_id=1, source_target_pairs={{0,4},{1,3},{2,6},{3,1},{4,0},{5,7},{6,2},{7,5},{8,12},{9,11},{10,... | collective-permute-start | bytes 1425416 | tf_op jit(solution)/shard_map/ppermute | solution.py:56
  138.3 4.4 %collective-permute-start.17 = (bf16[32,3712]{1,0:T(8,128)(2,1)S(1)}, bf16[32,3712]{1,0:T(8,128)(2,1)S(1)}, u32[]{:S(2)}, u32[]{:S(2)}) collective-permute-start(bf16[32,3712]{1,0:T(8,128)(2,1)S(1)} %get-tuple-element.45), channel_id=1, source_target_pairs={{0,1},{1,0},{2,3},{3,2},{4,5},{5,4},{6,7},{7,6},{8,9},{9,8},{10,11... | collective-permute-start | bytes 712712 | tf_op jit(solution)/shard_map/ppermute | solution.py:56
  141.4 3.7 %collective-permute-start.14 = (bf16[32,3712]{1,0:T(8,128)(2,1)S(1)}, bf16[32,3712]{1,0:T(8,128)(2,1)S(1)}, u32[]{:S(2)}, u32[]{:S(2)}) collective-permute-start(bf16[32,3712]{1,0:T(8,128)(2,1)S(1)} %get-tuple-element.43), channel_id=1, source_target_pairs={{0,1},{1,0},{2,3},{3,2},{4,5},{5,4},{6,7},{7,6},{8,9},{9,8},{10,11... | collective-permute-start | bytes 712712 | tf_op jit(solution)/shard_map/ppermute | solution.py:56
  143.8 2.5 %collective-permute-start.20 = (bf16[32,3712]{1,0:T(8,128)(2,1)S(1)}, bf16[32,3712]{1,0:T(8,128)(2,1)S(1)}, u32[]{:S(2)}, u32[]{:S(2)}) collective-permute-start(bf16[32,3712]{1,0:T(8,128)(2,1)S(1)} %get-tuple-element.47), channel_id=1, source_target_pairs={{0,1},{1,0},{2,3},{3,2},{4,5},{5,4},{6,7},{7,6},{8,9},{9,8},{10,11... | collective-permute-start | bytes 712712 | tf_op jit(solution)/shard_map/ppermute | solution.py:56
  146.7 1.2 copy-start.5
  146.7 2.3 %copy-start.1 = (bf16[128,3584]{1,0:T(8,128)(2,1)S(1)}, bf16[128,3584]{1,0:T(8,128)(2,1)}, u32[]{:S(2)}) copy-start(bf16[128,3584]{1,0:T(8,128)(2,1)} %param.7) | copy-start | bytes 2752516

commit v4 on v2

--- a/solution.py
+++ b/solution.py
@@ -1,6 +1,10 @@
+import functools
+
 import jax
 import jax.numpy as jnp
 from jax import lax
+from jax.experimental import pallas as pl
+from jax.experimental.pallas import tpu as pltpu
 from jax.sharding import PartitionSpec as P
 
 SHARDS = 4
@@ -34,6 +38,103 @@
         column == 0, high[:, None], jnp.where(column == 1, (prob - high)[:, None], 0.0)
     )
     return jnp.concatenate([rows.astype(jnp.bfloat16), tail.astype(jnp.bfloat16)], axis=1)
+
+
+def gather_rows(mine, other, x, g):
+    sources, _, cap, _ = mine.shape
+    for j in range(sources):
+        for k, ref in ((0, mine), (1, other)):
+            rows = slice((k * sources + j) * cap, (k * sources + j + 1) * cap)
+            x[rows, :] = ref[j, 0]
+            g[rows, :] = ref[j, 1]
+
+
+def forward_and_grads(x, g, pairs, grads):
+    total = 0.0
+    for i, (two, one) in enumerate(pairs):
+        units = one.shape[0]
+        forward = times(x[...], two[...])
+        ret = times_transposed(g[...], one[...])
+        gate, up = forward[:, :units], forward[:, units:]
+        act, slope = silu_parts(gate)
+        total += jnp.sum(act * up * ret, axis=1, keepdims=True)
+        grads[i, :, :units] = (ret * up * slope).astype(jnp.bfloat16)
+        grads[i, :, units:] = (ret * act).astype(jnp.bfloat16)
+    return total
+
+
+def first_kernel(mine, other, both, down, sums, probs, x, g, grads):
+    gather_rows(mine, other, x, g)
+    total = forward_and_grads(x, g, ((both, down),), grads)
+    sums[...] = times_transposed(grads[0], both[...])
+    probs[...] = jnp.broadcast_to(total, probs.shape)
+
+
+def last_kernel(before, *refs):
+    mine, other, refs = refs[0], refs[1], refs[2:]
+    if before:
+        sums, probs, refs = refs[0], refs[1], refs[2:]
+    *weights, part, prob, theirs, x, g, grads = refs
+    pairs = tuple(zip(weights[::2], weights[1::2]))
+    half, width = part.shape
+    gather_rows(mine, other, x, g)
+    total = forward_and_grads(x, g, pairs, grads)
+    out = sums[...] if before else 0.0
+    for i, (two, _) in enumerate(pairs):
+        out += times_transposed(grads[i], two[...])
+    if before:
+        total += probs[:, :1]
+    part[...] = out[:half]
+    theirs[:, :width] = out[half:].astype(jnp.bfloat16)
+    prob[...] = jnp.broadcast_to(total[:half], prob.shape)
+    high = total[half:].astype(jnp.bfloat16).astype(jnp.float32)
+    column = lax.broadcasted_iota(jnp.int32, (half, LANES), 1)
+    tail = jnp.where(column == 0, high, jnp.where(column == 1, total[half:] - high, 0.0))
+    theirs[:, width:] = tail.astype(jnp.bfloat16)
+
+
+def call(kernel, out_shape, mine, operands, count, name):
+    sources, _, cap, width = mine.shape
+    rows, units = 2 * sources * cap, operands[-1].shape[0]
+    vmem = pl.BlockSpec(memory_space=pltpu.VMEM)
+    return pl.pallas_call(
+        kernel,
+        out_shape=out_shape,
+        in_specs=[vmem] * (1 + len(operands)),
+        out_specs=(vmem,) * len(out_shape),
+        scratch_shapes=[
+            pltpu.VMEM((rows, width), jnp.bfloat16),
+            pltpu.VMEM((rows, width), jnp.bfloat16),
+            pltpu.VMEM((count, rows, 2 * units), jnp.bfloat16),
+        ],
+        compiler_params=pltpu.CompilerParams(vmem_limit_bytes=28 * 2**20),
+        cost_estimate=pl.CostEstimate(
+            flops=2000000001 * count, bytes_accessed=1, transcendentals=0
+        ),
+        name=name,
+    )(mine, *operands)
+
+
+def first_sums(mine, other, both_w, down_w):
+    rows, width = 2 * mine.shape[0] * mine.shape[2], mine.shape[3]
+    out_shape = (
+        jax.ShapeDtypeStruct((rows, width), jnp.float32),
+        jax.ShapeDtypeStruct((rows, LANES), jnp.float32),
+    )
+    return call(first_kernel, out_shape, mine, (other, both_w, down_w), 1, "first_sums")
+
+
+def chunk_sums(mine, other, *operands):
+    before = operands[0].dtype == jnp.float32
+    half, width = mine.shape[0] * mine.shape[2], mine.shape[3]
+    out_shape = (
+        jax.ShapeDtypeStruct((half, width), jnp.float32),
+        jax.ShapeDtypeStruct((half, LANES), jnp.float32),
+        jax.ShapeDtypeStruct((half, width + LANES), jnp.bfloat16),
+    )
+    kernel = functools.partial(last_kernel, before)
+    count = len(operands) // 2 - int(before)
+    return call(kernel, out_shape, mine, (other,) + operands, count, "chunk_sums")
 
 
 def shards(tokens, grad_out, expert_ids, combine, w_gate, w_up, w_down):
@@ -102,7 +203,7 @@
         if k == 0:
             arrived.append(merged[i])
         else:
-            chunk = merged[i] if i < 2 else tie(merged[i], arrived[i - 2])
+            chunk = merged[i] if i < 2 else tie(merged[i], arrived[0])
             arrived.append(send(chunk, k, 0))
 
     swapped = [None] * blocks
@@ -112,19 +213,16 @@
 
     def compute(i, *wait):
         mine, other = arrived[i], tie(swapped[i], *wait)
-        x = jnp.concatenate([mine[:, 0].reshape(half, width), other[:, 0].reshape(half, width)])
-        g = jnp.concatenate([mine[:, 1].reshape(half, width), other[:, 1].reshape(half, width)])
-        partial, prob = 0.0, 0.0
-        for forward_w, down_w in ((both_w, w_down[0]), (both_in, down_in)):
-            forward = times(x, forward_w)
-            gate, up = forward[:, :units], forward[:, units:]
-            back = times_transposed(g, down_w)
-            act, slope = silu_parts(gate)
-            prob = prob + jnp.sum(act * up * back, axis=1)
-            grads = jnp.concatenate([back * up * slope, back * act], axis=1).astype(jnp.bfloat16)
-            partial = partial + times_transposed(grads, forward_w)
-        theirs = with_prob(partial[half:], prob[half:])
-        return partial[:half], prob[:half], theirs
+        if cap % 16:
+            mine, other = (
+                value.swapaxes(0, 1).reshape(1, 2, half, width) for value in (mine, other)
+            )
+        if i == 0:
+            sums = first_sums(mine, other, both_w, w_down[0])
+            part, prob, theirs = chunk_sums(mine, other, *sums, both_in, down_in)
+        else:
+            part, prob, theirs = chunk_sums(mine, other, both_w, w_down[0], both_in, down_in)
+        return part, prob[:, 0], theirs
 
     def finish(i, part, *wait):
         partial, prob, theirs = part
@@ -134,30 +232,34 @@
         )
         return total
 
+    own = blocks - 1
+    final = own - 1
     parts = [None] * blocks
     totals = [None] * blocks
-    swap_in(0)
+    swap_in(0, arrived[1])
     swap_in(1)
-    for first in range(0, blocks, 2):
-        last = min(first + 1, blocks - 1)
-        for i in range(first, last + 1):
-            wait = [parts[i - 1][2]] if i > first else []
-            if i == first and i > 0:
-                wait.append(totals[i - 1])
-            parts[i] = compute(i, *wait)
-            if i == first:
-                for j in range(last + 1, min(last + 3, blocks)):
-                    swap_in(j, parts[i][2], arrived[min(last + 1, blocks - 1)])
-        for i in range(first, last + 1):
-            totals[i] = finish(i, parts[i], parts[last][2])
-
+    parts[0] = compute(0)
+    totals[0] = finish(0, parts[0], arrived[2], swapped[1])
+    for i in range(1, final):
+        parts[i] = compute(i, totals[i - 1])
+        swap_in(i + 1, parts[i - 1][2])
+        if i + 1 < final:
+            totals[i] = finish(i, parts[i])
+    parts[final] = compute(final, parts[final - 1][2])
+    totals[final - 1] = finish(final - 1, parts[final - 1], parts[final][2])
+    totals[final] = finish(final, parts[final])
+    swap_in(own, parts[final][2])
+    parts[own] = compute(own, totals[final])
+    totals[own] = finish(own, parts[own])
+
+    select = select.T.reshape(count, blocks, half).astype(jnp.bfloat16)
     rows = 0.0
-    select = select.T.reshape(count, blocks, half).astype(jnp.bfloat16)
     for i in range(blocks):
         total = totals[i] if order[i] == 0 else give_back(totals[i], order[i], 0)
         parts_in = [total[:cap]]
         for m in range(1, narrow):
-            parts_in.append(give_back(total[m * cap : (m + 1) * cap], 0, m))
+            piece = total[m * cap : (m + 1) * cap]
+            parts_in.append(give_back(piece, 0, m))
         rows = rows + times(select[:, i], jnp.concatenate(parts_in, axis=0))
     token_grad = (combine[:, None] * rows[:, :width]).astype(jnp.bfloat16)
     prob_grad = rows[:, width] + rows[:, width + 1]

time: 164 us -> 152 us (0.927)
  Pallas kernels: 0 us -> 22.5 us
  matrix products: 25.2 us -> 3.16 us
  waiting for transfers between devices: 105 us -> 91.3 us
    pallas_call x0 -> x5, Pallas kernels: none -> 22.5 us  [call(): pl.pallas_call(kernel, out_shape=out_shape, in_specs=[vmem] * (1 + len(op...]
    dot_general x16 -> x0, matrix products: 17 us -> none  [times_transposed(): lax.dot_general(left, right, (((1,), (1,)), ((), ())), preferred_element_...]
    ppermute x21, waiting for transfers between devices: 105 us -> 91.3 us  [permute(): return lax.ppermute(value, AXES, pairs)]
    dot_general x14 -> x6, matrix products: 8.23 us -> 3.16 us  [times(): return jnp.dot(left, right, preferred_element_type=jnp.float32)]
  transfers between devices with their start and end apart: 21 -> 21, of which waited for: 12 -> 13; matrix products, arithmetic and copies ran while one was open for 17% -> 3% of each run, Pallas kernels for 0% -> 15%
where the time goes in v4:
time: 152 us; the launch traced here: 150 us
  waiting for transfers between devices  91.3 us (60%)
  starting transfers between devices  24.1 us (16%)
  Pallas kernels  22.5 us (15%)
  other arithmetic  6.55 us (4%)
  matrix products  3.16 us (2%)
  local copies, waits for them, and re-layouts  1.55 us (1%)
    ppermute x21, waiting for transfers between devices, permute(): return lax.ppermute(value, AXES, pairs)  91.3 us
    ppermute x21, starting transfers between devices, permute(): return lax.ppermute(value, AXES, pairs)  24.1 us
    pallas_call x5, Pallas kernels, call(): pl.pallas_call(kernel, out_shape=out_shape, in_specs=[vmem] * (1 + len(op...  22.5 us
    dot_general x6, matrix products, times(): return jnp.dot(left, right, preferred_element_type=jnp.float32)  3.16 us
  transfers between devices with their start and end apart: 21, of which 13 were waited for; matrix products, arithmetic and copies ran while one was open for 3% of the time, Pallas kernels for 15%

profile of v4, /device:TPU:19, one launch (start us, length us, event | category | flops | bytes accessed | tf_op | source)
XLA Modules:
  0.0 150.2 jit_solution(11089312974549089479)
XLA Ops:
  0.7 0.9 convert_reduce_fusion
  4.0 0.7 collective-permute-start
  6.2 1.3 collective-permute-start.4
  8.9 1.3 collective-permute-start.2
  10.2 1.2 collective-permute-start.5
  11.4 36.5 %collective-permute-done.1.mine.refs_0_ = bf16[2,2,32,3584]{3,2,1,0:T(8,128)(2,1)S(1)} collective-permute-done((bf16[2,2,32,3584]{3,2,1,0:T(8,128)(2,1)S(1)}, bf16[2,2,32,3584]{3,2,1,0:T(8,128)(2,1)S(1)}, u32[]{:S(2)}, u32[]{:S(2)}) %collective-permute-start.1) | collective-permute-done | bytes 917536 | tf_op jit(solution)/shard_map/ppermute | solution.py:157
  47.9 2.0 %collective-permute-done.2.refs_0_ = bf16[2,2,32,3584]{3,2,1,0:T(8,128)(2,1)S(1)} collective-permute-done((bf16[2,2,32,3584]{3,2,1,0:T(8,128)(2,1)S(1)}, bf16[2,2,32,3584]{3,2,1,0:T(8,128)(2,1)S(1)}, u32[]{:S(2)}, u32[]{:S(2)}) %collective-permute-start.2) | collective-permute-done | bytes 917536 | tf_op jit(solution)/shard_map/ppermute | solution.py:157
  50.2 1.3 collective-permute-start.7
  51.5 1.3 collective-permute-start.8
  52.7 19.7 %collective-permute-done.3.other.refs_1_ = bf16[2,2,32,3584]{3,2,1,0:T(8,128)(2,1)S(1)} collective-permute-done((bf16[2,2,32,3584]{3,2,1,0:T(8,128)(2,1)S(1)}, bf16[2,2,32,3584]{3,2,1,0:T(8,128)(2,1)S(1)}, u32[]{:S(2)}, u32[]{:S(2)}) %collective-permute-start.3) | collective-permute-done | bytes 917536 | tf_op jit(solution)/shard_map/ppermute | solution.py:157
  72.4 3.1 %first_sums.1 = (f32[128,3584]{1,0:T(8,128)S(1)}, f32[128,128]{1,0:T(8,128)S(1)}) custom-call(bf16[2,2,32,3584]{3,2,1,0:T(8,128)(2,1)S(1)} %collective-permute-done.1.mine.refs_0_, bf16[2,2,32,3584]{3,2,1,0:T(8,128)(2,1)S(1)} %collective-permute-done.3.other.refs_1_, bf16[3584,512]{1,0:T(8,128)(2,1)S(1)} %pad_maximum_fusion.both.refs_2_, ...), custom_call_target="tpu_custom_call" | custom-call | flops 2000000000 | bytes 1 | tf_op jit(solution)/shard_map/first_sums/pallas_call | solution.py:100
  75.5 6.0 %collective-permute-done.5.refs_5_ = bf16[256,3584]{1,0:T(8,128)(2,1)S(1)} collective-permute-done((bf16[256,3584]{1,0:T(8,128)(2,1)S(1)}, bf16[256,3584]{1,0:T(8,128)(2,1)S(1)}, u32[]{:S(2)}, u32[]{:S(2)}) %collective-permute-start.5) | collective-permute-done | bytes 1835040 | tf_op jit(solution)/shard_map/ppermute | solution.py:157
  81.5 3.1 %chunk_sums.4 = (f32[64,3584]{1,0:T(8,128)S(1)}, f32[64,128]{1,0:T(8,128)S(1)}, bf16[64,3712]{1,0:T(8,128)(2,1)S(1)}) custom-call(bf16[2,2,32,3584]{3,2,1,0:T(8,128)(2,1)S(1)} %collective-permute-done.1.mine.refs_0_, bf16[2,2,32,3584]{3,2,1,0:T(8,128)(2,1)S(1)} %collective-permute-done.3.other.refs_1_, f32[128,3584]{1,0:T(8,128)S(1)} %get-tuple-element.26.refs_2_, ...), custom_call_target="tpu_custom_call" | custom-call | flops 2000000000 | bytes 1 | tf_op jit(solution)/shard_map/chunk_sums/pallas_call | solution.py:100
  85.0 4.8 %collective-permute-done.7.refs_0_ = bf16[2,2,32,3584]{3,2,1,0:T(8,128)(2,1)S(1)} collective-permute-done((bf16[2,2,32,3584]{3,2,1,0:T(8,128)(2,1)S(1)}, bf16[2,2,32,3584]{3,2,1,0:T(8,128)(2,1)S(1)}, u32[]{:S(2)}, u32[]{:S(2)}) %collective-permute-start.7) | collective-permute-done | bytes 917536 | tf_op jit(solution)/shard_map/ppermute | solution.py:157
  89.8 1.7 %collective-permute-start.12 = (bf16[2,2,32,3584]{3,2,1,0:T(8,128)(2,1)S(1)}, bf16[2,2,32,3584]{3,2,1,0:T(8,128)(2,1)S(1)}, u32[]{:S(2)}, u32[]{:S(2)}) collective-permute-start(bf16[2,2,32,3584]{3,2,1,0:T(8,128)(2,1)S(1)} %collective-permute-done.7.refs_0_), channel_id=1, source_target_pairs={{0,4},{1,3},{2,6},{3,1},{4,0},{5,7},{6,2},{7,5},{8,12},{9,11},{10,... | collective-permute-start | bytes 2752520 | tf_op jit(solution)/shard_map/ppermute | solution.py:157
  91.4 2.4 %collective-permute-done.6 = bf16[64,3712]{1,0:T(8,128)(2,1)S(1)} collective-permute-done((bf16[64,3712]{1,0:T(8,128)(2,1)S(1)}, bf16[64,3712]{1,0:T(8,128)(2,1)S(1)}, u32[]{:S(2)}, u32[]{:S(2)}) %collective-permute-start.6) | collective-permute-done | bytes 475168 | tf_op jit(solution)/shard_map/ppermute | solution.py:157
  94.4 5.4 %chunk_sums.5 = (f32[64,3584]{1,0:T(8,128)S(1)}, f32[64,128]{1,0:T(8,128)S(1)}, bf16[64,3712]{1,0:T(8,128)(2,1)S(1)}) custom-call(bf16[2,2,32,3584]{3,2,1,0:T(8,128)(2,1)S(1)} %collective-permute-done.2.refs_0_, bf16[2,2,32,3584]{3,2,1,0:T(8,128)(2,1)S(1)} %collective-permute-done.8.refs_1_, bf16[3584,512]{1,0:T(8,128)(2,1)S(1)} %pad_maximum_fusion.both.refs_2_, ...), custom_call_target="tpu_custom_call" | custom-call | flops 4000000000 | bytes 1 | tf_op jit(solution)/shard_map/chunk_sums/pallas_call | solution.py:100
  100.3 3.4 %collective-permute-done.12.refs_1_ = bf16[2,2,32,3584]{3,2,1,0:T(8,128)(2,1)S(1)} collective-permute-done((bf16[2,2,32,3584]{3,2,1,0:T(8,128)(2,1)S(1)}, bf16[2,2,32,3584]{3,2,1,0:T(8,128)(2,1)S(1)}, u32[]{:S(2)}, u32[]{:S(2)}) %collective-permute-start.12) | collective-permute-done | bytes 917536 | tf_op jit(solution)/shard_map/ppermute | solution.py:157
  103.7 5.4 %chunk_sums.6 = (f32[64,3584]{1,0:T(8,128)S(1)}, f32[64,128]{1,0:T(8,128)S(1)}, bf16[64,3712]{1,0:T(8,128)(2,1)S(1)}) custom-call(bf16[2,2,32,3584]{3,2,1,0:T(8,128)(2,1)S(1)} %collective-permute-done.7.refs_0_, bf16[2,2,32,3584]{3,2,1,0:T(8,128)(2,1)S(1)} %collective-permute-done.12.refs_1_, bf16[3584,512]{1,0:T(8,128)(2,1)S(1)} %pad_maximum_fusion.both.refs_2_, ...), custom_call_target="tpu_custom_call" | custom-call | flops 4000000000 | bytes 1 | tf_op jit(solution)/shard_map/chunk_sums/pallas_call | solution.py:100
  109.5 1.2 collective-permute-start.18
  110.7 3.4 %collective-permute-done.9 = bf16[64,3712]{1,0:T(8,128)(2,1)S(1)} collective-permute-done((bf16[64,3712]{1,0:T(8,128)(2,1)S(1)}, bf16[64,3712]{1,0:T(8,128)(2,1)S(1)}, u32[]{:S(2)}, u32[]{:S(2)}) %collective-permute-start.9) | collective-permute-done | bytes 475168 | tf_op jit(solution)/shard_map/ppermute | solution.py:157
  114.2 1.6 %collective-permute-start.10 = (bf16[32,3712]{1,0:T(8,128)(2,1)S(1)}, bf16[32,3712]{1,0:T(8,128)(2,1)S(1)}, u32[]{:S(2)}, u32[]{:S(2)}) collective-permute-start(bf16[32,3712]{1,0:T(8,128)(2,1)S(1)} %get-tuple-element.63), channel_id=1, source_target_pairs={{0,1},{1,0},{2,3},{3,2},{4,5},{5,4},{6,7},{7,6},{8,9},{9,8},{10,11... | collective-permute-start | bytes 712712 | tf_op jit(solution)/shard_map/ppermute | solution.py:157
  116.1 0.9 collective-permute-done.15
  117.5 1.5 %collective-permute-start.16 = (bf16[64,3712]{1,0:T(8,128)(2,1)S(1)}, bf16[64,3712]{1,0:T(8,128)(2,1)S(1)}, u32[]{:S(2)}, u32[]{:S(2)}) collective-permute-start(bf16[64,3712]{1,0:T(8,128)(2,1)S(1)} %pad_maximum_fusion.5), channel_id=1, source_target_pairs={{0,24},{1,25},{2,26},{3,27},{4,28},{5,29},{6,30},{7,31},{8,16},{9,... | collective-permute-start | bytes 1425416 | tf_op jit(solution)/shard_map/ppermute | solution.py:157
  119.2 2.0 %collective-permute-start.13 = (bf16[64,3712]{1,0:T(8,128)(2,1)S(1)}, bf16[64,3712]{1,0:T(8,128)(2,1)S(1)}, u32[]{:S(2)}, u32[]{:S(2)}) collective-permute-start(bf16[64,3712]{1,0:T(8,128)(2,1)S(1)} %pad_maximum_fusion.4), channel_id=1, source_target_pairs={{0,8},{1,9},{2,10},{3,11},{4,12},{5,13},{6,14},{7,15},{8,0},{9,1},... | collective-permute-start | bytes 1425416 | tf_op jit(solution)/shard_map/ppermute | solution.py:157
  121.3 5.5 %collective-permute-done.18.refs_1_ = bf16[2,2,32,3584]{3,2,1,0:T(8,128)(2,1)S(1)} collective-permute-done((bf16[2,2,32,3584]{3,2,1,0:T(8,128)(2,1)S(1)}, bf16[2,2,32,3584]{3,2,1,0:T(8,128)(2,1)S(1)}, u32[]{:S(2)}, u32[]{:S(2)}) %collective-permute-start.18) | collective-permute-done | bytes 917536 | tf_op jit(solution)/shard_map/ppermute | solution.py:157
  126.8 5.4 %chunk_sums.7 = (f32[64,3584]{1,0:T(8,128)S(1)}, f32[64,128]{1,0:T(8,128)S(1)}, bf16[64,3712]{1,0:T(8,128)(2,1)S(1)}) custom-call(bf16[2,2,32,3584]{3,2,1,0:T(8,128)(2,1)S(1)} %get-tuple-element.43.refs_0_, bf16[2,2,32,3584]{3,2,1,0:T(8,128)(2,1)S(1)} %collective-permute-done.18.refs_1_, bf16[3584,512]{1,0:T(8,128)(2,1)S(1)} %pad_maximum_fusion.both.refs_2_, ...), custom_call_target="tpu_custom_call" | custom-call | flops 4000000000 | bytes 1 | tf_op jit(solution)/shard_map/chunk_sums/pallas_call | solution.py:100
  132.6 5.4 %collective-permute-done.16 = bf16[64,3712]{1,0:T(8,128)(2,1)S(1)} collective-permute-done((bf16[64,3712]{1,0:T(8,128)(2,1)S(1)}, bf16[64,3712]{1,0:T(8,128)(2,1)S(1)}, u32[]{:S(2)}, u32[]{:S(2)}) %collective-permute-start.16) | collective-permute-done | bytes 475168 | tf_op jit(solution)/shard_map/ppermute | solution.py:157
  138.0 3.1 %collective-permute-start.17 = (bf16[32,3712]{1,0:T(8,128)(2,1)S(1)}, bf16[32,3712]{1,0:T(8,128)(2,1)S(1)}, u32[]{:S(2)}, u32[]{:S(2)}) collective-permute-start(bf16[32,3712]{1,0:T(8,128)(2,1)S(1)} %get-tuple-element.67), channel_id=1, source_target_pairs={{0,1},{1,0},{2,3},{3,2},{4,5},{5,4},{6,7},{7,6},{8,9},{9,8},{10,11... | collective-permute-start | bytes 712712 | tf_op jit(solution)/shard_map/ppermute | solution.py:157
  141.1 2.0 %collective-permute-start.14 = (bf16[32,3712]{1,0:T(8,128)(2,1)S(1)}, bf16[32,3712]{1,0:T(8,128)(2,1)S(1)}, u32[]{:S(2)}, u32[]{:S(2)}) collective-permute-start(bf16[32,3712]{1,0:T(8,128)(2,1)S(1)} %get-tuple-element.65), channel_id=1, source_target_pairs={{0,1},{1,0},{2,3},{3,2},{4,5},{5,4},{6,7},{7,6},{8,9},{9,8},{10,11... | collective-permute-start | bytes 712712 | tf_op jit(solution)/shard_map/ppermute | solution.py:157
  144.1 2.1 %collective-permute-start.20 = (bf16[32,3712]{1,0:T(8,128)(2,1)S(1)}, bf16[32,3712]{1,0:T(8,128)(2,1)S(1)}, u32[]{:S(2)}, u32[]{:S(2)}) collective-permute-start(bf16[32,3712]{1,0:T(8,128)(2,1)S(1)} %get-tuple-element.69), channel_id=1, source_target_pairs={{0,1},{1,0},{2,3},{3,2},{4,5},{5,4},{6,7},{7,6},{8,9},{9,8},{10,11... | collective-permute-start | bytes 712712 | tf_op jit(solution)/shard_map/ppermute | solution.py:157
  149.1 1.1 fusion.3
  (69 shorter events, 12.3 us)
Async XLA Ops:
  0.6 1.6 %copy-start = (bf16[128,3584]{1,0:T(8,128)(2,1)S(1)}, bf16[128,3584]{1,0:T(8,128)(2,1)}, u32[]{:S(2)}) copy-start(bf16[128,3584]{1,0:T(8,128)(2,1)} %param.7) | copy-start | bytes 2752516
  0.6 2.2 %copy-start.5 = (bf16[128,3584]{1,0:T(8,128)(2,1)S(1)}, bf16[128,3584]{1,0:T(8,128)(2,1)}, u32[]{:S(2)}) copy-start(bf16[128,3584]{1,0:T(8,128)(2,1)} %param.8) | copy-start | bytes 2752516
  3.8 1.5 %copy-start.3 = (bf16[1,3584,256]{2,1,0:T(8,128)(2,1)S(1)}, bf16[1,3584,256]{2,1,0:T(8,128)(2,1)}, u32[]{:S(2)}) copy-start(bf16[1,3584,256]{2,1,0:T(8,128)(2,1)} %param.12) | copy-start | bytes 5505028
  3.9 2.0 %copy-start.4 = (bf16[1,3584,256]{2,1,0:T(8,128)(2,1)S(1)}, bf16[1,3584,256]{2,1,0:T(8,128)(2,1)}, u32[]{:S(2)}) copy-start(bf16[1,3584,256]{2,1,0:T(8,128)(2,1)} %param.11) | copy-start | bytes 5505028
  4.0 4.2 %collective-permute-start = (bf16[4,2,32,3584]{3,2,1,0:T(8,128)(2,1)S(1)}, bf16[4,2,32,3584]{3,2,1,0:T(8,128)(2,1)S(1)}, u32[]{:S(2)}, u32[]{:S(2)}) collective-permute-start(bf16[4,2,32,3584]{3,2,1,0:T(8,128)(2,1)S(1)} %bitcast.45), channel_id=1, source_target_pairs={{0,1},{1,0},{2,3},{3,2},{4,5},{5,4},{6,7},{7,6},{8,9},{9,8},{10,11... | collective-permute-start | bytes 5505032 | tf_op jit(solution)/shard_map/ppermute | solution.py:157
  6.2 75.3 %collective-permute-start.4 = (bf16[3584,512]{1,0:T(8,128)(2,1)S(1)}, bf16[3584,512]{1,0:T(8,128)(2,1)S(1)}, u32[]{:S(2)}, u32[]{:S(2)}) collective-permute-start(bf16[3584,512]{1,0:T(8,128)(2,1)S(1)} %pad_maximum_fusion.both.refs_2_), channel_id=1, source_target_pairs={{0,2},{1,5},{2,0},{3,7},{4,6},{5,1},{6,4},{7,3},{8,10},{9,13},{10,... | collective-permute-start | bytes 11010056 | tf_op jit(solution)/shard_map/ppermute | solution.py:157
  8.2 2.0 %copy-start.2 = (bf16[1,256,3584]{2,1,0:T(8,128)(2,1)S(1)}, bf16[1,256,3584]{2,1,0:T(8,128)(2,1)}, u32[]{:S(2)}) copy-start(bf16[1,256,3584]{2,1,0:T(8,128)(2,1)} %param.13) | copy-start | bytes 5505028
  8.7 39.2 %collective-permute-start.1 = (bf16[2,2,32,3584]{3,2,1,0:T(8,128)(2,1)S(1)}, bf16[2,2,32,3584]{3,2,1,0:T(8,128)(2,1)S(1)}, u32[]{:S(2)}, u32[]{:S(2)}) collective-permute-start(bf16[2,2,32,3584]{3,2,1,0:T(8,128)(2,1)S(1)} %get-tuple-element.57), channel_id=1, source_target_pairs={{0,16},{1,17},{2,18},{3,19},{4,20},{5,21},{6,22},{7,23},{8,24},{9,... | collective-permute-start | bytes 2752520 | tf_op jit(solution)/shard_map/ppermute | solution.py:157
  8.9 41.1 %collective-permute-start.2 = (bf16[2,2,32,3584]{3,2,1,0:T(8,128)(2,1)S(1)}, bf16[2,2,32,3584]{3,2,1,0:T(8,128)(2,1)S(1)}, u32[]{:S(2)}, u32[]{:S(2)}) collective-permute-start(bf16[2,2,32,3584]{3,2,1,0:T(8,128)(2,1)S(1)} %get-tuple-element.56), channel_id=1, source_target_pairs={{0,8},{1,9},{2,10},{3,11},{4,12},{5,13},{6,14},{7,15},{8,0},{9,1},... | collective-permute-start | bytes 2752520 | tf_op jit(solution)/shard_map/ppermute | solution.py:157
  10.2 71.3 %collective-permute-start.5 = (bf16[256,3584]{1,0:T(8,128)(2,1)S(1)}, bf16[256,3584]{1,0:T(8,128)(2,1)S(1)}, u32[]{:S(2)}, u32[]{:S(2)}) collective-permute-start(bf16[256,3584]{1,0:T(8,128)(2,1)S(1)} %bitcast.34), channel_id=1, source_target_pairs={{0,2},{1,5},{2,0},{3,7},{4,6},{5,1},{6,4},{7,3},{8,10},{9,13},{10,... | collective-permute-start | bytes 5505032 | tf_op jit(solution)/shard_map/ppermute | solution.py:157
  50.0 22.4 %collective-permute-start.3 = (bf16[2,2,32,3584]{3,2,1,0:T(8,128)(2,1)S(1)}, bf16[2,2,32,3584]{3,2,1,0:T(8,128)(2,1)S(1)}, u32[]{:S(2)}, u32[]{:S(2)}) collective-permute-start(bf16[2,2,32,3584]{3,2,1,0:T(8,128)(2,1)S(1)} %collective-permute-done.1.mine.refs_0_), channel_id=1, source_target_pairs={{0,4},{1,3},{2,6},{3,1},{4,0},{5,7},{6,2},{7,5},{8,12},{9,11},{10,... | collective-permute-start | bytes 2752520 | tf_op jit(solution)/shard_map/ppermute | solution.py:157
  50.2 39.6 %collective-permute-start.7 = (bf16[2,2,32,3584]{3,2,1,0:T(8,128)(2,1)S(1)}, bf16[2,2,32,3584]{3,2,1,0:T(8,128)(2,1)S(1)}, u32[]{:S(2)}, u32[]{:S(2)}) collective-permute-start(bf16[2,2,32,3584]{3,2,1,0:T(8,128)(2,1)S(1)} %get-tuple-element.30), channel_id=1, source_target_pairs={{0,24},{1,25},{2,26},{3,27},{4,28},{5,29},{6,30},{7,31},{8,16},{9,... | collective-permute-start | bytes 2752520 | tf_op jit(solution)/shard_map/ppermute | solution.py:157
  51.5 40.0 %collective-permute-start.8 = (bf16[2,2,32,3584]{3,2,1,0:T(8,128)(2,1)S(1)}, bf16[2,2,32,3584]{3,2,1,0:T(8,128)(2,1)S(1)}, u32[]{:S(2)}, u32[]{:S(2)}) collective-permute-start(bf16[2,2,32,3584]{3,2,1,0:T(8,128)(2,1)S(1)} %collective-permute-done.2.refs_0_), channel_id=1, source_target_pairs={{0,4},{1,3},{2,6},{3,1},{4,0},{5,7},{6,2},{7,5},{8,12},{9,11},{10,... | collective-permute-start | bytes 2752520 | tf_op jit(solution)/shard_map/ppermute | solution.py:157
  84.7 9.2 %collective-permute-start.6 = (bf16[64,3712]{1,0:T(8,128)(2,1)S(1)}, bf16[64,3712]{1,0:T(8,128)(2,1)S(1)}, u32[]{:S(2)}, u32[]{:S(2)}) collective-permute-start(bf16[64,3712]{1,0:T(8,128)(2,1)S(1)} %get-tuple-element.29), channel_id=1, source_target_pairs={{0,4},{1,3},{2,6},{3,1},{4,0},{5,7},{6,2},{7,5},{8,12},{9,11},{10,... | collective-permute-start | bytes 1425416 | tf_op jit(solution)/shard_map/ppermute | solution.py:157
  89.8 13.9 %collective-permute-start.12 = (bf16[2,2,32,3584]{3,2,1,0:T(8,128)(2,1)S(1)}, bf16[2,2,32,3584]{3,2,1,0:T(8,128)(2,1)S(1)}, u32[]{:S(2)}, u32[]{:S(2)}) collective-permute-start(bf16[2,2,32,3584]{3,2,1,0:T(8,128)(2,1)S(1)} %collective-permute-done.7.refs_0_), channel_id=1, source_target_pairs={{0,4},{1,3},{2,6},{3,1},{4,0},{5,7},{6,2},{7,5},{8,12},{9,11},{10,... | collective-permute-start | bytes 2752520 | tf_op jit(solution)/shard_map/ppermute | solution.py:157
  94.3 19.8 %collective-permute-start.9 = (bf16[64,3712]{1,0:T(8,128)(2,1)S(1)}, bf16[64,3712]{1,0:T(8,128)(2,1)S(1)}, u32[]{:S(2)}, u32[]{:S(2)}) collective-permute-start(bf16[64,3712]{1,0:T(8,128)(2,1)S(1)} %pad_maximum_fusion.3), channel_id=1, source_target_pairs={{0,16},{1,17},{2,18},{3,19},{4,20},{5,21},{6,22},{7,23},{8,24},{9,... | collective-permute-start | bytes 1425416 | tf_op jit(solution)/shard_map/ppermute | solution.py:157
  99.9 10.8 %collective-permute-start.11 = (bf16[64,3712]{1,0:T(8,128)(2,1)S(1)}, bf16[64,3712]{1,0:T(8,128)(2,1)S(1)}, u32[]{:S(2)}, u32[]{:S(2)}) collective-permute-start(bf16[64,3712]{1,0:T(8,128)(2,1)S(1)} %get-tuple-element.35), channel_id=1, source_target_pairs={{0,4},{1,3},{2,6},{3,1},{4,0},{5,7},{6,2},{7,5},{8,12},{9,11},{10,... | collective-permute-start | bytes 1425416 | tf_op jit(solution)/shard_map/ppermute | solution.py:157
  109.1 7.9 %collective-permute-start.15 = (bf16[64,3712]{1,0:T(8,128)(2,1)S(1)}, bf16[64,3712]{1,0:T(8,128)(2,1)S(1)}, u32[]{:S(2)}, u32[]{:S(2)}) collective-permute-start(bf16[64,3712]{1,0:T(8,128)(2,1)S(1)} %get-tuple-element.38), channel_id=1, source_target_pairs={{0,4},{1,3},{2,6},{3,1},{4,0},{5,7},{6,2},{7,5},{8,12},{9,11},{10,... | collective-permute-start | bytes 1425416 | tf_op jit(solution)/shard_map/ppermute | solution.py:157
  109.5 17.3 %collective-permute-start.18 = (bf16[2,2,32,3584]{3,2,1,0:T(8,128)(2,1)S(1)}, bf16[2,2,32,3584]{3,2,1,0:T(8,128)(2,1)S(1)}, u32[]{:S(2)}, u32[]{:S(2)}) collective-permute-start(bf16[2,2,32,3584]{3,2,1,0:T(8,128)(2,1)S(1)} %get-tuple-element.43.refs_0_), channel_id=1, source_target_pairs={{0,4},{1,3},{2,6},{3,1},{4,0},{5,7},{6,2},{7,5},{8,12},{9,11},{10,... | collective-permute-start | bytes 2752520 | tf_op jit(solution)/shard_map/ppermute | solution.py:157
  114.2 33.6 %collective-permute-start.10 = (bf16[32,3712]{1,0:T(8,128)(2,1)S(1)}, bf16[32,3712]{1,0:T(8,128)(2,1)S(1)}, u32[]{:S(2)}, u32[]{:S(2)}) collective-permute-start(bf16[32,3712]{1,0:T(8,128)(2,1)S(1)} %get-tuple-element.63), channel_id=1, source_target_pairs={{0,1},{1,0},{2,3},{3,2},{4,5},{5,4},{6,7},{7,6},{8,9},{9,8},{10,11... | collective-permute-start | bytes 712712 | tf_op jit(solution)/shard_map/ppermute | solution.py:157
  117.5 20.5 %collective-permute-start.16 = (bf16[64,3712]{1,0:T(8,128)(2,1)S(1)}, bf16[64,3712]{1,0:T(8,128)(2,1)S(1)}, u32[]{:S(2)}, u32[]{:S(2)}) collective-permute-start(bf16[64,3712]{1,0:T(8,128)(2,1)S(1)} %pad_maximum_fusion.5), channel_id=1, source_target_pairs={{0,24},{1,25},{2,26},{3,27},{4,28},{5,29},{6,30},{7,31},{8,16},{9,... | collective-permute-start | bytes 1425416 | tf_op jit(solution)/shard_map/ppermute | solution.py:157
  119.2 21.9 %collective-permute-start.13 = (bf16[64,3712]{1,0:T(8,128)(2,1)S(1)}, bf16[64,3712]{1,0:T(8,128)(2,1)S(1)}, u32[]{:S(2)}, u32[]{:S(2)}) collective-permute-start(bf16[64,3712]{1,0:T(8,128)(2,1)S(1)} %pad_maximum_fusion.4), channel_id=1, source_target_pairs={{0,8},{1,9},{2,10},{3,11},{4,12},{5,13},{6,14},{7,15},{8,0},{9,1},... | collective-permute-start | bytes 1425416 | tf_op jit(solution)/shard_map/ppermute | solution.py:157
  132.2 11.4 %collective-permute-start.19 = (bf16[64,3712]{1,0:T(8,128)(2,1)S(1)}, bf16[64,3712]{1,0:T(8,128)(2,1)S(1)}, u32[]{:S(2)}, u32[]{:S(2)}) collective-permute-start(bf16[64,3712]{1,0:T(8,128)(2,1)S(1)} %get-tuple-element.46), channel_id=1, source_target_pairs={{0,4},{1,3},{2,6},{3,1},{4,0},{5,7},{6,2},{7,5},{8,12},{9,11},{10,... | collective-permute-start | bytes 1425416 | tf_op jit(solution)/shard_map/ppermute | solution.py:157
  138.0 5.1 %collective-permute-start.17 = (bf16[32,3712]{1,0:T(8,128)(2,1)S(1)}, bf16[32,3712]{1,0:T(8,128)(2,1)S(1)}, u32[]{:S(2)}, u32[]{:S(2)}) collective-permute-start(bf16[32,3712]{1,0:T(8,128)(2,1)S(1)} %get-tuple-element.67), channel_id=1, source_target_pairs={{0,1},{1,0},{2,3},{3,2},{4,5},{5,4},{6,7},{7,6},{8,9},{9,8},{10,11... | collective-permute-start | bytes 712712 | tf_op jit(solution)/shard_map/ppermute | solution.py:157
  141.1 5.1 %collective-permute-start.14 = (bf16[32,3712]{1,0:T(8,128)(2,1)S(1)}, bf16[32,3712]{1,0:T(8,128)(2,1)S(1)}, u32[]{:S(2)}, u32[]{:S(2)}) collective-permute-start(bf16[32,3712]{1,0:T(8,128)(2,1)S(1)} %get-tuple-element.65), channel_id=1, source_target_pairs={{0,1},{1,0},{2,3},{3,2},{4,5},{5,4},{6,7},{7,6},{8,9},{9,8},{10,11... | collective-permute-start | bytes 712712 | tf_op jit(solution)/shard_map/ppermute | solution.py:157
  144.1 3.2 %collective-permute-start.20 = (bf16[32,3712]{1,0:T(8,128)(2,1)S(1)}, bf16[32,3712]{1,0:T(8,128)(2,1)S(1)}, u32[]{:S(2)}, u32[]{:S(2)}) collective-permute-start(bf16[32,3712]{1,0:T(8,128)(2,1)S(1)} %get-tuple-element.69), channel_id=1, source_target_pairs={{0,1},{1,0},{2,3},{3,2},{4,5},{5,4},{6,7},{7,6},{8,9},{9,8},{10,11... | collective-permute-start | bytes 712712 | tf_op jit(solution)/shard_map/ppermute | solution.py:157
  147.8 1.3 copy-start.6
  147.8 2.3 %copy-start.1 = (bf16[128,3584]{1,0:T(8,128)(2,1)S(1)}, bf16[128,3584]{1,0:T(8,128)(2,1)}, u32[]{:S(2)}) copy-start(bf16[128,3584]{1,0:T(8,128)(2,1)} %param.7) | copy-start | bytes 2752516

commit v5 on v3

--- a/solution.py
+++ b/solution.py
@@ -93,10 +93,14 @@
         axis=2,
     )
 
-    turned = [
-        permute(packed[:, m], lambda b, s, c: (b, s, (c + m) % narrow)) for m in range(1, narrow)
-    ]
-    merged = jnp.stack([packed[:, 0]] + turned, axis=1)
+    merged = []
+    for lot in (slice(0, 2), slice(2, blocks)):
+        turned = [
+            permute(packed[lot, m], lambda b, s, c: (b, s, (c + m) % narrow))
+            for m in range(1, narrow)
+        ]
+        lots = jnp.stack([packed[lot, 0]] + turned, axis=1)
+        merged += [lots[i] for i in range(lots.shape[0])]
     arrived = []
     for i, k in enumerate(order):
         if k == 0:

time: 151 us -> 151 us (level)
    ppermute x21 -> x22, starting transfers between devices: 22.2 us -> 22.2 us  [permute(): return lax.ppermute(value, AXES, pairs)]
    ppermute x21 -> x22, waiting for transfers between devices: 91.5 us -> 91.5 us  [permute(): return lax.ppermute(value, AXES, pairs)]
  transfers between devices with their start and end apart: 21 -> 22, of which waited for: 11 -> 11; matrix products, arithmetic and copies ran while one was open for 19% -> 18% of each run, Pallas kernels for 0% -> 0%
where the time goes in v5:
time: 151 us; the launch traced here: 149 us
  waiting for transfers between devices  91.5 us (61%)
  matrix products  25.1 us (17%)
  starting transfers between devices  22.2 us (15%)
  other arithmetic  7.05 us (5%)
  local copies, waits for them, and re-layouts  1.65 us (1%)
    ppermute x22, waiting for transfers between devices, permute(): return lax.ppermute(value, AXES, pairs)  91.5 us
    ppermute x22, starting transfers between devices, permute(): return lax.ppermute(value, AXES, pairs)  22.2 us
    dot_general x16, matrix products, times_transposed(): lax.dot_general(left, right, (((1,), (1,)), ((), ())), preferred_element_...  16.8 us
    dot_general x14, matrix products, times(): return jnp.dot(left, right, preferred_element_type=jnp.float32)  8.23 us
  transfers between devices with their start and end apart: 22, of which 11 were waited for; matrix products, arithmetic and copies ran while one was open for 18% of the time, Pallas kernels for 0%

profile of v5, /device:TPU:19, one launch (start us, length us, event | category | flops | bytes accessed | tf_op | source)
XLA Modules:
  0.0 148.8 jit_solution(13968921748632487109)
XLA Ops:
  0.7 0.9 convert_reduce_fusion
  5.9 1.3 collective-permute-start.4
  7.2 1.1 collective-permute-start.3
  8.7 1.3 collective-permute-start.10
  10.3 37.6 %collective-permute-done.1 = bf16[2,2,32,3584]{3,2,1,0:T(8,128)(2,1)S(1)} collective-permute-done((bf16[2,2,32,3584]{3,2,1,0:T(8,128)(2,1)S(1)}, bf16[2,2,32,3584]{3,2,1,0:T(8,128)(2,1)S(1)}, u32[]{:S(2)}, u32[]{:S(2)}) %collective-permute-start.1) | collective-permute-done | bytes 917536 | tf_op jit(solution)/shard_map/ppermute | solution.py:56
  47.9 2.9 %collective-permute-start.7 = (bf16[2,2,32,3584]{3,2,1,0:T(8,128)(2,1)S(1)}, bf16[2,2,32,3584]{3,2,1,0:T(8,128)(2,1)S(1)}, u32[]{:S(2)}, u32[]{:S(2)}) collective-permute-start(bf16[2,2,32,3584]{3,2,1,0:T(8,128)(2,1)S(1)} %get-tuple-element.10), channel_id=1, source_target_pairs={{0,24},{1,25},{2,26},{3,27},{4,28},{5,29},{6,30},{7,31},{8,16},{9,... | collective-permute-start | bytes 2752520 | tf_op jit(solution)/shard_map/ppermute | solution.py:56
  51.0 1.2 collective-permute-start.11
  52.4 20.8 %collective-permute-done.2 = bf16[2,2,32,3584]{3,2,1,0:T(8,128)(2,1)S(1)} collective-permute-done((bf16[2,2,32,3584]{3,2,1,0:T(8,128)(2,1)S(1)}, bf16[2,2,32,3584]{3,2,1,0:T(8,128)(2,1)S(1)}, u32[]{:S(2)}, u32[]{:S(2)}) %collective-permute-start.2) | collective-permute-done | bytes 917536 | tf_op jit(solution)/shard_map/ppermute | solution.py:56
  74.7 1.3 fusion.52
  76.7 3.7 %collective-permute-done.3 = bf16[256,3584]{1,0:T(8,128)(2,1)S(1)} collective-permute-done((bf16[256,3584]{1,0:T(8,128)(2,1)S(1)}, bf16[256,3584]{1,0:T(8,128)(2,1)S(1)}, u32[]{:S(2)}, u32[]{:S(2)}) %collective-permute-start.3) | collective-permute-done | bytes 1835040 | tf_op jit(solution)/shard_map/ppermute | solution.py:56
  81.3 1.3 convolution_add_fusion.3
  83.2 7.6 %collective-permute-done.7 = bf16[2,2,32,3584]{3,2,1,0:T(8,128)(2,1)S(1)} collective-permute-done((bf16[2,2,32,3584]{3,2,1,0:T(8,128)(2,1)S(1)}, bf16[2,2,32,3584]{3,2,1,0:T(8,128)(2,1)S(1)}, u32[]{:S(2)}, u32[]{:S(2)}) %collective-permute-start.7) | collective-permute-done | bytes 917536 | tf_op jit(solution)/shard_map/ppermute | solution.py:56
  91.1 2.4 %collective-permute-done.5 = bf16[64,3712]{1,0:T(8,128)(2,1)S(1)} collective-permute-done((bf16[64,3712]{1,0:T(8,128)(2,1)S(1)}, bf16[64,3712]{1,0:T(8,128)(2,1)S(1)}, u32[]{:S(2)}, u32[]{:S(2)}) %collective-permute-start.5) | collective-permute-done | bytes 475168 | tf_op jit(solution)/shard_map/ppermute | solution.py:56
  95.7 1.3 fusion.59
  98.4 1.3 convolution_add_fusion.2
  100.3 3.1 %collective-permute-done.13 = bf16[2,2,32,3584]{3,2,1,0:T(8,128)(2,1)S(1)} collective-permute-done((bf16[2,2,32,3584]{3,2,1,0:T(8,128)(2,1)S(1)}, bf16[2,2,32,3584]{3,2,1,0:T(8,128)(2,1)S(1)}, u32[]{:S(2)}, u32[]{:S(2)}) %collective-permute-start.13) | collective-permute-done | bytes 917536 | tf_op jit(solution)/shard_map/ppermute | solution.py:56
  106.5 1.3 fusion.66
  107.8 1.3 convolution_add_fusion.1
  109.6 1.3 collective-permute-start.19
  111.0 2.8 %collective-permute-done.8 = bf16[64,3712]{1,0:T(8,128)(2,1)S(1)} collective-permute-done((bf16[64,3712]{1,0:T(8,128)(2,1)S(1)}, bf16[64,3712]{1,0:T(8,128)(2,1)S(1)}, u32[]{:S(2)}, u32[]{:S(2)}) %collective-permute-start.8) | collective-permute-done | bytes 475168 | tf_op jit(solution)/shard_map/ppermute | solution.py:56
  113.9 1.6 %collective-permute-start.9 = (bf16[32,3712]{1,0:T(8,128)(2,1)S(1)}, bf16[32,3712]{1,0:T(8,128)(2,1)S(1)}, u32[]{:S(2)}, u32[]{:S(2)}) collective-permute-start(bf16[32,3712]{1,0:T(8,128)(2,1)S(1)} %get-tuple-element.43), channel_id=1, source_target_pairs={{0,1},{1,0},{2,3},{3,2},{4,5},{5,4},{6,7},{7,6},{8,9},{9,8},{10,11... | collective-permute-start | bytes 712712 | tf_op jit(solution)/shard_map/ppermute | solution.py:56
  115.7 1.4 collective-permute-done.16
  117.7 1.2 collective-permute-start.17
  118.9 1.8 %collective-permute-start.14 = (bf16[64,3712]{1,0:T(8,128)(2,1)S(1)}, bf16[64,3712]{1,0:T(8,128)(2,1)S(1)}, u32[]{:S(2)}, u32[]{:S(2)}) collective-permute-start(bf16[64,3712]{1,0:T(8,128)(2,1)S(1)} %pad_maximum_fusion.32), channel_id=1, source_target_pairs={{0,8},{1,9},{2,10},{3,11},{4,12},{5,13},{6,14},{7,15},{8,0},{9,1},... | collective-permute-start | bytes 1425416 | tf_op jit(solution)/shard_map/ppermute | solution.py:56
  120.7 6.3 %collective-permute-done.19 = bf16[2,2,32,3584]{3,2,1,0:T(8,128)(2,1)S(1)} collective-permute-done((bf16[2,2,32,3584]{3,2,1,0:T(8,128)(2,1)S(1)}, bf16[2,2,32,3584]{3,2,1,0:T(8,128)(2,1)S(1)}, u32[]{:S(2)}, u32[]{:S(2)}) %collective-permute-start.19) | collective-permute-done | bytes 917536 | tf_op jit(solution)/shard_map/ppermute | solution.py:56
  130.0 1.3 fusion.73
  131.3 1.3 convolution_add_fusion
  133.1 5.0 %collective-permute-done.17 = bf16[64,3712]{1,0:T(8,128)(2,1)S(1)} collective-permute-done((bf16[64,3712]{1,0:T(8,128)(2,1)S(1)}, bf16[64,3712]{1,0:T(8,128)(2,1)S(1)}, u32[]{:S(2)}, u32[]{:S(2)}) %collective-permute-start.17) | collective-permute-done | bytes 475168 | tf_op jit(solution)/shard_map/ppermute | solution.py:56
  138.2 3.1 %collective-permute-start.18 = (bf16[32,3712]{1,0:T(8,128)(2,1)S(1)}, bf16[32,3712]{1,0:T(8,128)(2,1)S(1)}, u32[]{:S(2)}, u32[]{:S(2)}) collective-permute-start(bf16[32,3712]{1,0:T(8,128)(2,1)S(1)} %get-tuple-element.47), channel_id=1, source_target_pairs={{0,1},{1,0},{2,3},{3,2},{4,5},{5,4},{6,7},{7,6},{8,9},{9,8},{10,11... | collective-permute-start | bytes 712712 | tf_op jit(solution)/shard_map/ppermute | solution.py:56
  141.3 1.4 collective-permute-start.15
  143.8 1.1 collective-permute-start.21
  147.7 1.1 fusion.2
  (121 shorter events, 24.7 us)
Async XLA Ops:
  0.6 1.6 %copy-start = (bf16[128,3584]{1,0:T(8,128)(2,1)S(1)}, bf16[128,3584]{1,0:T(8,128)(2,1)}, u32[]{:S(2)}) copy-start(bf16[128,3584]{1,0:T(8,128)(2,1)} %param.7) | copy-start | bytes 2752516
  0.6 2.2 %copy-start.4 = (bf16[128,3584]{1,0:T(8,128)(2,1)S(1)}, bf16[128,3584]{1,0:T(8,128)(2,1)}, u32[]{:S(2)}) copy-start(bf16[128,3584]{1,0:T(8,128)(2,1)} %param.8) | copy-start | bytes 2752516
  3.5 1.5 %copy-start.2 = (bf16[1,3584,256]{2,1,0:T(8,128)(2,1)S(1)}, bf16[1,3584,256]{2,1,0:T(8,128)(2,1)}, u32[]{:S(2)}) copy-start(bf16[1,3584,256]{2,1,0:T(8,128)(2,1)} %param.12) | copy-start | bytes 5505028
  3.5 2.0 %copy-start.3 = (bf16[1,3584,256]{2,1,0:T(8,128)(2,1)S(1)}, bf16[1,3584,256]{2,1,0:T(8,128)(2,1)}, u32[]{:S(2)}) copy-start(bf16[1,3584,256]{2,1,0:T(8,128)(2,1)} %param.11) | copy-start | bytes 5505028
  3.9 6.1 %collective-permute-start.6 = (bf16[2,2,32,3584]{3,2,0,1:T(8,128)(2,1)S(1)}, bf16[2,2,32,3584]{3,2,0,1:T(8,128)(2,1)S(1)}, u32[]{:S(2)}, u32[]{:S(2)}) collective-permute-start(bf16[2,2,32,3584]{3,2,0,1:T(8,128)(2,1)S(1)} %get-tuple-element.20), channel_id=1, source_target_pairs={{0,1},{1,0},{2,3},{3,2},{4,5},{5,4},{6,7},{7,6},{8,9},{9,8},{10,11... | collective-permute-start | bytes 2752520 | tf_op jit(solution)/shard_map/ppermute | solution.py:56
  4.7 3.8 %collective-permute-start = (bf16[2,2,32,3584]{3,2,0,1:T(8,128)(2,1)S(1)}, bf16[2,2,32,3584]{3,2,0,1:T(8,128)(2,1)S(1)}, u32[]{:S(2)}, u32[]{:S(2)}) collective-permute-start(bf16[2,2,32,3584]{3,2,0,1:T(8,128)(2,1)S(1)} %get-tuple-element.18), channel_id=1, source_target_pairs={{0,1},{1,0},{2,3},{3,2},{4,5},{5,4},{6,7},{7,6},{8,9},{9,8},{10,11... | collective-permute-start | bytes 2752520 | tf_op jit(solution)/shard_map/ppermute | solution.py:56
  5.6 1.6 %copy-start.6 = (bf16[1,256,3584]{2,1,0:T(8,128)(2,1)S(1)}, bf16[1,256,3584]{2,1,0:T(8,128)(2,1)}, u32[]{:S(2)}) copy-start(bf16[1,256,3584]{2,1,0:T(8,128)(2,1)} %param.13) | copy-start | bytes 5505028
  5.9 70.2 %collective-permute-start.4 = (bf16[3584,512]{1,0:T(8,128)(2,1)S(1)}, bf16[3584,512]{1,0:T(8,128)(2,1)S(1)}, u32[]{:S(2)}, u32[]{:S(2)}) collective-permute-start(bf16[3584,512]{1,0:T(8,128)(2,1)S(1)} %pad_maximum_fusion), channel_id=1, source_target_pairs={{0,2},{1,5},{2,0},{3,7},{4,6},{5,1},{6,4},{7,3},{8,10},{9,13},{10,... | collective-permute-start | bytes 11010056 | tf_op jit(solution)/shard_map/ppermute | solution.py:56
  7.2 73.3 %collective-permute-start.3 = (bf16[256,3584]{1,0:T(8,128)(2,1)S(1)}, bf16[256,3584]{1,0:T(8,128)(2,1)S(1)}, u32[]{:S(2)}, u32[]{:S(2)}) collective-permute-start(bf16[256,3584]{1,0:T(8,128)(2,1)S(1)} %bitcast.135), channel_id=1, source_target_pairs={{0,2},{1,5},{2,0},{3,7},{4,6},{5,1},{6,4},{7,3},{8,10},{9,13},{10,... | collective-permute-start | bytes 5505032 | tf_op jit(solution)/shard_map/ppermute | solution.py:56
  8.6 39.2 %collective-permute-start.1 = (bf16[2,2,32,3584]{3,2,1,0:T(8,128)(2,1)S(1)}, bf16[2,2,32,3584]{3,2,1,0:T(8,128)(2,1)S(1)}, u32[]{:S(2)}, u32[]{:S(2)}) collective-permute-start(bf16[2,2,32,3584]{3,2,1,0:T(8,128)(2,1)S(1)} %get-tuple-element.23), channel_id=1, source_target_pairs={{0,16},{1,17},{2,18},{3,19},{4,20},{5,21},{6,22},{7,23},{8,24},{9,... | collective-permute-start | bytes 2752520 | tf_op jit(solution)/shard_map/ppermute | solution.py:56
  8.7 42.3 %collective-permute-start.10 = (bf16[2,2,32,3584]{3,2,1,0:T(8,128)(2,1)S(1)}, bf16[2,2,32,3584]{3,2,1,0:T(8,128)(2,1)S(1)}, u32[]{:S(2)}, u32[]{:S(2)}) collective-permute-start(bf16[2,2,32,3584]{3,2,1,0:T(8,128)(2,1)S(1)} %get-tuple-element.22), channel_id=1, source_target_pairs={{0,8},{1,9},{2,10},{3,11},{4,12},{5,13},{6,14},{7,15},{8,0},{9,1},... | collective-permute-start | bytes 2752520 | tf_op jit(solution)/shard_map/ppermute | solution.py:56
  47.9 42.9 %collective-permute-start.7 = (bf16[2,2,32,3584]{3,2,1,0:T(8,128)(2,1)S(1)}, bf16[2,2,32,3584]{3,2,1,0:T(8,128)(2,1)S(1)}, u32[]{:S(2)}, u32[]{:S(2)}) collective-permute-start(bf16[2,2,32,3584]{3,2,1,0:T(8,128)(2,1)S(1)} %get-tuple-element.10), channel_id=1, source_target_pairs={{0,24},{1,25},{2,26},{3,27},{4,28},{5,29},{6,30},{7,31},{8,16},{9,... | collective-permute-start | bytes 2752520 | tf_op jit(solution)/shard_map/ppermute | solution.py:56
  50.8 22.4 %collective-permute-start.2 = (bf16[2,2,32,3584]{3,2,1,0:T(8,128)(2,1)S(1)}, bf16[2,2,32,3584]{3,2,1,0:T(8,128)(2,1)S(1)}, u32[]{:S(2)}, u32[]{:S(2)}) collective-permute-start(bf16[2,2,32,3584]{3,2,1,0:T(8,128)(2,1)S(1)} %collective-permute-done.1), channel_id=1, source_target_pairs={{0,4},{1,3},{2,6},{3,1},{4,0},{5,7},{6,2},{7,5},{8,12},{9,11},{10,... | collective-permute-start | bytes 2752520 | tf_op jit(solution)/shard_map/ppermute | solution.py:56
  51.0 43.1 %collective-permute-start.11 = (bf16[2,2,32,3584]{3,2,1,0:T(8,128)(2,1)S(1)}, bf16[2,2,32,3584]{3,2,1,0:T(8,128)(2,1)S(1)}, u32[]{:S(2)}, u32[]{:S(2)}) collective-permute-start(bf16[2,2,32,3584]{3,2,1,0:T(8,128)(2,1)S(1)} %collective-permute-done.10), channel_id=1, source_target_pairs={{0,4},{1,3},{2,6},{3,1},{4,0},{5,7},{6,2},{7,5},{8,12},{9,11},{10,... | collective-permute-start | bytes 2752520 | tf_op jit(solution)/shard_map/ppermute | solution.py:56
  82.9 10.7 %collective-permute-start.5 = (bf16[64,3712]{1,0:T(8,128)(2,1)S(1)}, bf16[64,3712]{1,0:T(8,128)(2,1)S(1)}, u32[]{:S(2)}, u32[]{:S(2)}) collective-permute-start(bf16[64,3712]{1,0:T(8,128)(2,1)S(1)} %pad_maximum_fusion.28), channel_id=1, source_target_pairs={{0,4},{1,3},{2,6},{3,1},{4,0},{5,7},{6,2},{7,5},{8,12},{9,11},{10,... | collective-permute-start | bytes 1425416 | tf_op jit(solution)/shard_map/ppermute | solution.py:56
  90.8 12.6 %collective-permute-start.13 = (bf16[2,2,32,3584]{3,2,1,0:T(8,128)(2,1)S(1)}, bf16[2,2,32,3584]{3,2,1,0:T(8,128)(2,1)S(1)}, u32[]{:S(2)}, u32[]{:S(2)}) collective-permute-start(bf16[2,2,32,3584]{3,2,1,0:T(8,128)(2,1)S(1)} %collective-permute-done.7), channel_id=1, source_target_pairs={{0,4},{1,3},{2,6},{3,1},{4,0},{5,7},{6,2},{7,5},{8,12},{9,11},{10,... | collective-permute-start | bytes 2752520 | tf_op jit(solution)/shard_map/ppermute | solution.py:56
  94.0 19.8 %collective-permute-start.8 = (bf16[64,3712]{1,0:T(8,128)(2,1)S(1)}, bf16[64,3712]{1,0:T(8,128)(2,1)S(1)}, u32[]{:S(2)}, u32[]{:S(2)}) collective-permute-start(bf16[64,3712]{1,0:T(8,128)(2,1)S(1)} %pad_maximum_fusion.29), channel_id=1, source_target_pairs={{0,16},{1,17},{2,18},{3,19},{4,20},{5,21},{6,22},{7,23},{8,24},{9,... | collective-permute-start | bytes 1425416 | tf_op jit(solution)/shard_map/ppermute | solution.py:56
  100.0 10.8 %collective-permute-start.12 = (bf16[64,3712]{1,0:T(8,128)(2,1)S(1)}, bf16[64,3712]{1,0:T(8,128)(2,1)S(1)}, u32[]{:S(2)}, u32[]{:S(2)}) collective-permute-start(bf16[64,3712]{1,0:T(8,128)(2,1)S(1)} %pad_maximum_fusion.30), channel_id=1, source_target_pairs={{0,4},{1,3},{2,6},{3,1},{4,0},{5,7},{6,2},{7,5},{8,12},{9,11},{10,... | collective-permute-start | bytes 1425416 | tf_op jit(solution)/shard_map/ppermute | solution.py:56
  109.3 7.9 %collective-permute-start.16 = (bf16[64,3712]{1,0:T(8,128)(2,1)S(1)}, bf16[64,3712]{1,0:T(8,128)(2,1)S(1)}, u32[]{:S(2)}, u32[]{:S(2)}) collective-permute-start(bf16[64,3712]{1,0:T(8,128)(2,1)S(1)} %pad_maximum_fusion.31), channel_id=1, source_target_pairs={{0,4},{1,3},{2,6},{3,1},{4,0},{5,7},{6,2},{7,5},{8,12},{9,11},{10,... | collective-permute-start | bytes 1425416 | tf_op jit(solution)/shard_map/ppermute | solution.py:56
  109.6 17.4 %collective-permute-start.19 = (bf16[2,2,32,3584]{3,2,1,0:T(8,128)(2,1)S(1)}, bf16[2,2,32,3584]{3,2,1,0:T(8,128)(2,1)S(1)}, u32[]{:S(2)}, u32[]{:S(2)}) collective-permute-start(bf16[2,2,32,3584]{3,2,1,0:T(8,128)(2,1)S(1)} %get-tuple-element.16), channel_id=1, source_target_pairs={{0,4},{1,3},{2,6},{3,1},{4,0},{5,7},{6,2},{7,5},{8,12},{9,11},{10,... | collective-permute-start | bytes 2752520 | tf_op jit(solution)/shard_map/ppermute | solution.py:56
  113.9 32.6 %collective-permute-start.9 = (bf16[32,3712]{1,0:T(8,128)(2,1)S(1)}, bf16[32,3712]{1,0:T(8,128)(2,1)S(1)}, u32[]{:S(2)}, u32[]{:S(2)}) collective-permute-start(bf16[32,3712]{1,0:T(8,128)(2,1)S(1)} %get-tuple-element.43), channel_id=1, source_target_pairs={{0,1},{1,0},{2,3},{3,2},{4,5},{5,4},{6,7},{7,6},{8,9},{9,8},{10,11... | collective-permute-start | bytes 712712 | tf_op jit(solution)/shard_map/ppermute | solution.py:56
  117.7 20.5 %collective-permute-start.17 = (bf16[64,3712]{1,0:T(8,128)(2,1)S(1)}, bf16[64,3712]{1,0:T(8,128)(2,1)S(1)}, u32[]{:S(2)}, u32[]{:S(2)}) collective-permute-start(bf16[64,3712]{1,0:T(8,128)(2,1)S(1)} %pad_maximum_fusion.33), channel_id=1, source_target_pairs={{0,24},{1,25},{2,26},{3,27},{4,28},{5,29},{6,30},{7,31},{8,16},{9,... | collective-permute-start | bytes 1425416 | tf_op jit(solution)/shard_map/ppermute | solution.py:56
  118.9 22.4 %collective-permute-start.14 = (bf16[64,3712]{1,0:T(8,128)(2,1)S(1)}, bf16[64,3712]{1,0:T(8,128)(2,1)S(1)}, u32[]{:S(2)}, u32[]{:S(2)}) collective-permute-start(bf16[64,3712]{1,0:T(8,128)(2,1)S(1)} %pad_maximum_fusion.32), channel_id=1, source_target_pairs={{0,8},{1,9},{2,10},{3,11},{4,12},{5,13},{6,14},{7,15},{8,0},{9,1},... | collective-permute-start | bytes 1425416 | tf_op jit(solution)/shard_map/ppermute | solution.py:56
  132.8 10.4 %collective-permute-start.20 = (bf16[64,3712]{1,0:T(8,128)(2,1)S(1)}, bf16[64,3712]{1,0:T(8,128)(2,1)S(1)}, u32[]{:S(2)}, u32[]{:S(2)}) collective-permute-start(bf16[64,3712]{1,0:T(8,128)(2,1)S(1)} %pad_maximum_fusion.34), channel_id=1, source_target_pairs={{0,4},{1,3},{2,6},{3,1},{4,0},{5,7},{6,2},{7,5},{8,12},{9,11},{10,... | collective-permute-start | bytes 1425416 | tf_op jit(solution)/shard_map/ppermute | solution.py:56
  138.2 4.6 %collective-permute-start.18 = (bf16[32,3712]{1,0:T(8,128)(2,1)S(1)}, bf16[32,3712]{1,0:T(8,128)(2,1)S(1)}, u32[]{:S(2)}, u32[]{:S(2)}) collective-permute-start(bf16[32,3712]{1,0:T(8,128)(2,1)S(1)} %get-tuple-element.47), channel_id=1, source_target_pairs={{0,1},{1,0},{2,3},{3,2},{4,5},{5,4},{6,7},{7,6},{8,9},{9,8},{10,11... | collective-permute-start | bytes 712712 | tf_op jit(solution)/shard_map/ppermute | solution.py:56
  141.3 3.5 %collective-permute-start.15 = (bf16[32,3712]{1,0:T(8,128)(2,1)S(1)}, bf16[32,3712]{1,0:T(8,128)(2,1)S(1)}, u32[]{:S(2)}, u32[]{:S(2)}) collective-permute-start(bf16[32,3712]{1,0:T(8,128)(2,1)S(1)} %get-tuple-element.45), channel_id=1, source_target_pairs={{0,1},{1,0},{2,3},{3,2},{4,5},{5,4},{6,7},{7,6},{8,9},{9,8},{10,11... | collective-permute-start | bytes 712712 | tf_op jit(solution)/shard_map/ppermute | solution.py:56
  143.8 2.2 %collective-permute-start.21 = (bf16[32,3712]{1,0:T(8,128)(2,1)S(1)}, bf16[32,3712]{1,0:T(8,128)(2,1)S(1)}, u32[]{:S(2)}, u32[]{:S(2)}) collective-permute-start(bf16[32,3712]{1,0:T(8,128)(2,1)S(1)} %get-tuple-element.49), channel_id=1, source_target_pairs={{0,1},{1,0},{2,3},{3,2},{4,5},{5,4},{6,7},{7,6},{8,9},{9,8},{10,11... | collective-permute-start | bytes 712712 | tf_op jit(solution)/shard_map/ppermute | solution.py:56
  146.5 1.2 copy-start.5
  146.5 2.3 %copy-start.1 = (bf16[128,3584]{1,0:T(8,128)(2,1)S(1)}, bf16[128,3584]{1,0:T(8,128)(2,1)}, u32[]{:S(2)}) copy-start(bf16[128,3584]{1,0:T(8,128)(2,1)} %param.7) | copy-start | bytes 2752516
